TPU v7x, 128 devices: a whole 4x4x4 slice. The times are simulated.
128 devices in a mesh: seq: 64 (over z, y, x_lo, core), batch: 2 (over x_hi).
Axes of the slice: x: 4 (x_hi: 2, x_lo: 2; x = x_hi * 2 + x_lo), y: 4, z: 4, core: 2. Of those that a mesh axis runs over, the one named last changes fastest.
Arguments:
- inputs: bfloat16 [4, 4096, 1536], P('batch', 'seq'), may hold values from -36 to 36
- conv_weight: bfloat16 [1536, 2304], P('seq'), may hold values from -0.09375 to 0.09375
- mix_weight: bfloat16 [768, 1536], P('seq'), may hold values from -0.21875 to 0.21875
- first_gain: float32 [1536], replicated, may hold values from 0.1 to 1.9
- first_bias: float32 [1536], replicated, may hold values from -3 to 3
- second_gain: float32 [768], replicated, may hold values from 0.1 to 1.9
- second_bias: float32 [768], replicated, may hold values from -3 to 3
- norm_gain: float32 [1536], replicated, may hold values from 0.1 to 1.9
- query_weight: bfloat16 [1536, 512], replicated, may hold values from -2.5 to 2.5
- key_weight: bfloat16 [1536, 512], replicated, may hold values from -2.5 to 2.5
- value_weight: bfloat16 [1536, 1536], replicated, may hold values from -0.4375 to 0.4375
- out_weight: bfloat16 [1536, 1536], replicated, may hold values from -0.15625 to 0.15625
- cotangent: bfloat16 [4, 4096, 1536], P('batch', 'seq'), may hold values from -12 to 12
Outputs:
- encoded: bfloat16 [4, 4096, 1536], P('batch', 'seq')
- grad_inputs: bfloat16 [4, 4096, 1536], P('batch', 'seq')
- grad_first_gain: float32 [1536], replicated
- grad_first_bias: float32 [1536], replicated
- grad_second_gain: float32 [768], replicated
- grad_second_bias: float32 [768], replicated
- grad_norm_gain: float32 [1536], replicated
All inputs are finite; a program needn't handle non-finite values.
Results may differ from a plain program's by a relative error of at most 0.04.
Values may be sent and summed in bfloat16 or wider, within the bound.
A program may use at most 192 MiB of HBM per device.

v0:
```python
import jax
import jax.numpy as jnp
from jax import lax
from jax.experimental import pallas as pl
from jax.experimental.pallas import tpu as pltpu
from jax.sharding import PartitionSpec as P

H = 8
KD = 64
VD = 192
DILATION_STEP = 16


EPS = 1e-05
GELU_C = 0.7978845608028654


MESH = pl.DeviceIdType.MESH


def seq_of(z, y, x, core):
    return ((z * 4 + y) * 2 + x) * 2 + core


def all_sum_kernel(x_ref, o_ref, line, plane, send_sem, recv_sem):
    seq = lax.axis_index("seq")
    batch = lax.axis_index("batch")
    mine = batch * 4 + lax.rem(seq, 4)
    spot = seq // 4

    def line_peer(step):
        other = lax.rem(mine + step, 8)
        return {"seq": spot * 4 + lax.rem(other, 4), "batch": other // 4}

    def plane_peer(step):
        return {"seq": lax.rem(spot + step, 16) * 4 + lax.rem(seq, 4), "batch": batch}

    barrier = pltpu.get_barrier_semaphore()
    for step in range(1, 8):
        pl.semaphore_signal(barrier, inc=1, device_id=line_peer(step), device_id_type=MESH)
    for step in range(1, 16):
        pl.semaphore_signal(barrier, inc=1, device_id=plane_peer(step), device_id_type=MESH)
    line[mine] = x_ref[...]
    pl.semaphore_wait(barrier, 22)

    copies = [
        pltpu.make_async_remote_copy(
            src_ref=x_ref,
            dst_ref=line.at[mine],
            send_sem=send_sem.at[step],
            recv_sem=recv_sem.at[step],
            device_id=line_peer(step),
            device_id_type=MESH,
        )
        for step in range(1, 8)
    ]
    for copy in copies:
        copy.start()
    for copy in copies:
        copy.wait()
    total = line[0]
    for i in range(1, 8):
        total = total + line[i]
    plane[spot] = total
    copies = [
        pltpu.make_async_remote_copy(
            src_ref=plane.at[spot],
            dst_ref=plane.at[spot],
            send_sem=send_sem.at[7 + step],
            recv_sem=recv_sem.at[7 + step],
            device_id=plane_peer(step),
            device_id_type=MESH,
        )
        for step in range(1, 16)
    ]
    for copy in copies:
        copy.start()
    for copy in copies:
        copy.wait()
    total = plane[0]
    for i in range(1, 16):
        total = total + plane[i]
    o_ref[...] = total


def all_sum(parts, number):
    width = parts[0].shape[0]
    joined = jnp.concatenate(parts).reshape(-1, 128)
    rows = joined.shape[0]
    full = -(-rows // 8) * 8
    if full != rows:
        joined = jnp.pad(joined, ((0, full - rows), (0, 0)))
    vmem = pl.BlockSpec(memory_space=pltpu.VMEM)
    summed = pl.pallas_call(
        all_sum_kernel,
        out_shape=jax.ShapeDtypeStruct((full, 128), jnp.float32),
        in_specs=[vmem],
        out_specs=vmem,
        scratch_shapes=[
            pltpu.VMEM((8, full, 128), jnp.float32),
            pltpu.VMEM((16, full, 128), jnp.float32),
            pltpu.SemaphoreType.DMA((23,)),
            pltpu.SemaphoreType.DMA((23,)),
        ],
        compiler_params=pltpu.CompilerParams(collective_id=number, has_side_effects=True),
        name=f"all_sum_{number}",
    )(joined)
    flat = summed.reshape(-1)
    return [flat[i * width : (i + 1) * width] for i in range(len(parts))]


def gather_kernel(conv_ref, mix_ref, conv_out, mix_out, send_sem, recv_sem, own_sem):
    seq = lax.axis_index("seq")
    core = lax.rem(seq, 2)
    x = lax.rem(seq // 2, 2)
    y = lax.rem(seq // 4, 4)
    z = seq // 16
    pairs = ((conv_ref, conv_out), (mix_ref, mix_out))

    def first_peer(step):
        return {"seq": seq_of(lax.rem(z + step * x, 4), lax.rem(y + step * (1 - x), 4), x, core)}

    def second_peer(step):
        return {"seq": seq_of(lax.rem(z + step * (1 - x), 4), lax.rem(y + step * x, 4), x, core)}

    def y_peer(step):
        return {"seq": seq_of(z, lax.rem(y + step, 4), x, core)}

    def z_peer(step):
        return {"seq": seq_of(lax.rem(z + step, 4), y, x, core)}

    x_peer = {"seq": seq_of(z, y, 1 - x, core)}
    sibling = {"seq": seq_of(z, y, x, 1 - core)}

    barrier = pltpu.get_barrier_semaphore()
    peers = [x_peer, sibling]
    for step in range(1, 4):
        peers += [y_peer(step), z_peer(step)]
    for peer in peers:
        pl.semaphore_signal(barrier, inc=1, device_id=peer, device_id_type=MESH)
    local = [
        pltpu.make_async_copy(source, out.at[z, y, x, core], own_sem.at[i])
        for i, (source, out) in enumerate(pairs)
    ]
    for copy in local:
        copy.start()
    pl.semaphore_wait(barrier, 8)

    def send(sources, targets, peer, slot):
        copies = [
            pltpu.make_async_remote_copy(
                src_ref=source,
                dst_ref=target,
                send_sem=send_sem.at[slot, i],
                recv_sem=recv_sem.at[slot, i],
                device_id=peer,
                device_id_type=MESH,
            )
            for i, (source, target) in enumerate(zip(sources, targets))
        ]
        for copy in copies:
            copy.start()
        return copies

    inputs = [conv_ref, mix_ref]
    outs = [conv_out, mix_out]
    own_place = [out.at[z, y, x, core] for out in outs]
    got_place = [out.at[z, y, 1 - x, core] for out in outs]
    started = []
    to_x = send(inputs, own_place, x_peer, 0)
    started += to_x
    spread = []
    for step in range(1, 4):
        spread += send(inputs, own_place, first_peer(step), step)
    for copy in to_x:
        copy.wait_recv()
    for step in range(1, 4):
        spread += send(got_place, got_place, second_peer(step), 3 + step)
    started += spread
    for copy in local:
        copy.wait()
    for copy in spread:
        copy.wait_recv()
    row_block = [out.at[z, :, 0, core] for out in outs]
    column_block = [out.at[:, y, 1, core] for out in outs]
    steps = []
    for step in (1, 3, 2):
        rows = send(row_block, row_block, z_peer(step), 6 + step)
        columns = send(column_block, column_block, y_peer(step), 9 + step)
        steps.append((step, rows, columns))
        started += rows + columns
    across = send(row_block, row_block, sibling, 13) + send(column_block, column_block, sibling, 14)
    for step, rows, columns in steps:
        for copy in rows:
            copy.wait_recv()
        block = [out.at[lax.rem(z + 4 - step, 4), :, 0, core] for out in outs]
        across += send(block, block, sibling, 14 + step)
        for copy in columns:
            copy.wait_recv()
        block = [out.at[:, lax.rem(y + 4 - step, 4), 1, core] for out in outs]
        across += send(block, block, sibling, 17 + step)
    for copy in across:
        copy.wait_recv()
    for copy in started + across:
        copy.wait_send()


def gather_weights(conv_weight, mix_weight):
    anywhere = pl.BlockSpec(memory_space=pl.ANY)
    conv_full, mix_full = pl.pallas_call(
        gather_kernel,
        out_shape=[
            jax.ShapeDtypeStruct((4, 4, 2, 2) + conv_weight.shape, conv_weight.dtype),
            jax.ShapeDtypeStruct((4, 4, 2, 2) + mix_weight.shape, mix_weight.dtype),
        ],
        in_specs=[anywhere, anywhere],
        out_specs=[anywhere, anywhere],
        scratch_shapes=[
            pltpu.SemaphoreType.DMA((21, 2)),
            pltpu.SemaphoreType.DMA((21, 2)),
            pltpu.SemaphoreType.DMA((2,)),
        ],
        compiler_params=pltpu.CompilerParams(collective_id=1, has_side_effects=True),
        name="gather_weights",
    )(conv_weight, mix_weight)
    return (
        conv_full.reshape(-1, conv_weight.shape[1]),
        mix_full.reshape(-1, mix_weight.shape[1]),
    )


LOW = VD
WIDE = VD + KD


def spots():
    seq = lax.axis_index("seq")
    core = lax.rem(seq, 2)
    z = seq // 16
    mine = (z // 2) * 8 + lax.rem(seq // 2, 8)
    return seq, core, lax.rem(z, 2), mine


def pair_ahead(mine, step):
    return lax.rem(mine // 4 + step // 4, 4) * 4 + lax.rem(lax.rem(mine, 4) + step % 4, 4)


def pair_behind(mine, step):
    return lax.rem(mine // 4 + 4 - step // 4, 4) * 4 + lax.rem(lax.rem(mine, 4) + 4 - step % 4, 4)


def holder(pair, z_low, core):
    return {"seq": ((pair // 8) * 2 + z_low) * 16 + lax.rem(pair, 8) * 2 + core}


def attention_peers(seq, core, z_low, mine):
    z_peer = {"seq": seq + 16 * (1 - 2 * z_low)}
    sibling = {"seq": seq + 1 - 2 * core}
    return z_peer, sibling


def greet(mine, z_low, core, z_peer, sibling):
    barrier = pltpu.get_barrier_semaphore()
    for step in range(1, 16):
        pl.semaphore_signal(
            barrier, inc=1, device_id=holder(pair_ahead(mine, step), z_low, core), device_id_type=MESH
        )
    pl.semaphore_signal(barrier, inc=1, device_id=z_peer, device_id_type=MESH)
    pl.semaphore_signal(barrier, inc=1, device_id=sibling, device_id_type=MESH)
    return barrier


def spread_kernel(q_ref, k_ref, v_ref, g_ref, x_out, y_out, x_part, y_part, send_sem, recv_sem):
    seq, core, z_low, mine = spots()
    z_peer, sibling = attention_peers(seq, core, z_low, mine)
    barrier = greet(mine, z_low, core, z_peer, sibling)
    for window in range(2):
        rows = slice(window * 64, window * 64 + 64)
        for head in range(H):
            pair = window * H + head
            y_part[pair, :, 0:LOW] = v_ref[rows, head * VD : head * VD + VD]
            y_part[pair, :, LOW:WIDE] = k_ref[rows, head * KD : head * KD + KD]
    pl.semaphore_wait(barrier, 17)

    def send(source, target, peer, slot):
        copy = pltpu.make_async_remote_copy(
            src_ref=source,
            dst_ref=target,
            send_sem=send_sem.at[slot],
            recv_sem=recv_sem.at[slot],
            device_id=peer,
            device_id_type=MESH,
        )
        copy.start()
        return copy

    y_sends = []
    for step in range(1, 16):
        pair = pair_ahead(mine, step)
        peer = holder(pair, z_low, core)
        y_sends.append(send(y_part.at[pair], y_out.at[z_low, core, mine], peer, step))
    for window in range(2):
        rows = slice(window * 64, window * 64 + 64)
        for head in range(H):
            pair = window * H + head
            x_part[pair, :, 0:LOW] = g_ref[rows, head * VD : head * VD + VD]
            x_part[pair, :, LOW:WIDE] = q_ref[rows, head * KD : head * KD + KD]
    x_sends = []
    for step in range(1, 16):
        pair = pair_ahead(mine, step)
        peer = holder(pair, z_low, core)
        x_sends.append(send(x_part.at[pair], x_out.at[mine], peer, 16 + step))
    y_out[z_low, core, mine] = y_part[mine]
    x_out[mine] = x_part[mine]
    along = []
    across = []
    for step in range(16):
        if step > 0:
            y_sends[step - 1].wait_recv()
        place = y_out.at[z_low, core, pair_behind(mine, step)]
        along.append(send(place, place, z_peer, 32 + step))
        across.append(send(place, place, sibling, 48 + step))
    for step in range(16):
        along[step].wait_recv()
        place = y_out.at[1 - z_low, core, pair_behind(mine, step)]
        across.append(send(place, place, sibling, 64 + step))
    for copy in x_sends + across:
        copy.wait_recv()
    for copy in y_sends + x_sends + along + across:
        copy.wait_send()


def spread(queries, keys, values, grad_out):
    vmem = pl.BlockSpec(memory_space=pltpu.VMEM)
    kind = queries.dtype
    return pl.pallas_call(
        spread_kernel,
        out_shape=[
            jax.ShapeDtypeStruct((16, 64, WIDE), kind),
            jax.ShapeDtypeStruct((2, 2, 16, 64, WIDE), kind),
        ],
        in_specs=[vmem] * 4,
        out_specs=[vmem] * 2,
        scratch_shapes=[
            pltpu.VMEM((16, 64, WIDE), kind),
            pltpu.VMEM((16, 64, WIDE), kind),
            pltpu.SemaphoreType.DMA((80,)),
            pltpu.SemaphoreType.DMA((80,)),
        ],
        compiler_params=pltpu.CompilerParams(
            collective_id=6, has_side_effects=True, vmem_limit_bytes=32 * 1024 * 1024
        ),
        name="spread",
    )(queries, keys, values, grad_out)


def collect_kernel(
    oq_ref, vk_ref, a_ref, gq_ref, gv_ref, gk_ref, oq_got, vk_got, from_core, to_z, from_z, total,
    send_sem, recv_sem
):
    seq, core, z_low, mine = spots()
    z_peer, sibling = attention_peers(seq, core, z_low, mine)
    barrier = greet(mine, z_low, core, z_peer, sibling)
    pl.semaphore_wait(barrier, 17)

    def send(source, target, peer, slot):
        copy = pltpu.make_async_remote_copy(
            src_ref=source,
            dst_ref=target,
            send_sem=send_sem.at[slot],
            recv_sem=recv_sem.at[slot],
            device_id=peer,
            device_id_type=MESH,
        )
        copy.start()
        return copy

    groups = [pl.ds(lax.rem(mine // 4 + k, 4) * 4, 4) for k in range(4)]
    across = []
    for far in range(2):
        z_part = 1 - z_low if far == 0 else z_low
        for k in range(4):
            across.append(
                send(
                    vk_ref.at[z_part, 1 - core, groups[k]],
                    from_core.at[far, groups[k]],
                    sibling,
                    4 * far + k,
                )
            )
    oq_sends = []
    for step in range(1, 16):
        pair = pair_ahead(mine, step)
        oq_sends.append(
            send(oq_ref.at[pair], oq_got.at[mine], holder(pair, z_low, core), 16 + step)
        )
    oq_got[mine] = oq_ref[mine]
    along = []
    for k in range(4):
        across[k].wait_recv()
        summed = vk_ref[1 - z_low, core, groups[k]].astype(jnp.float32) + from_core[
            0, groups[k]
        ].astype(jnp.float32)
        to_z[groups[k]] = summed.astype(to_z.dtype)
        along.append(send(to_z.at[groups[k]], from_z.at[groups[k]], z_peer, 8 + k))
    vk_sends = []
    for k in range(4):
        across[4 + k].wait_recv()
        along[k].wait_recv()
        summed = vk_ref[z_low, core, groups[k]].astype(jnp.float32) + from_core[
            1, groups[k]
        ].astype(jnp.float32)
        summed = summed + from_z[groups[k]].astype(jnp.float32)
        total[groups[k]] = summed.astype(total.dtype)
        for step in range(4 * k, 4 * k + 4):
            if step > 0:
                pair = pair_ahead(mine, step)
                vk_sends.append(
                    send(total.at[pair], vk_got.at[mine], holder(pair, z_low, core), 32 + step)
                )
    vk_got[mine] = total[mine]
    for copy in oq_sends:
        copy.wait_recv()
    for window in range(2):
        rows = slice(window * 64, window * 64 + 64)
        for head in range(H):
            pair = window * H + head
            a_ref[rows, head * VD : head * VD + VD] = oq_got[pair, :, 0:LOW]
            gq_ref[rows, head * KD : head * KD + KD] = oq_got[pair, :, LOW:WIDE]
    for copy in vk_sends:
        copy.wait_recv()
    for window in range(2):
        rows = slice(window * 64, window * 64 + 64)
        for head in range(H):
            pair = window * H + head
            gv_ref[rows, head * VD : head * VD + VD] = vk_got[pair, :, 0:LOW]
            gk_ref[rows, head * KD : head * KD + KD] = vk_got[pair, :, LOW:WIDE]
    for copy in across + oq_sends + along + vk_sends:
        copy.wait_send()


def collect(oq, vk):
    vmem = pl.BlockSpec(memory_space=pltpu.VMEM)
    kind = oq.dtype
    piece = (16, 64, WIDE)
    return pl.pallas_call(
        collect_kernel,
        out_shape=[
            jax.ShapeDtypeStruct((128, H * VD), kind),
            jax.ShapeDtypeStruct((128, H * KD), kind),
            jax.ShapeDtypeStruct((128, H * VD), kind),
            jax.ShapeDtypeStruct((128, H * KD), kind),
        ],
        in_specs=[vmem] * 2,
        out_specs=[vmem] * 4,
        scratch_shapes=[
            pltpu.VMEM(piece, kind),
            pltpu.VMEM(piece, kind),
            pltpu.VMEM((2,) + piece, kind),
            pltpu.VMEM(piece, kind),
            pltpu.VMEM(piece, kind),
            pltpu.VMEM(piece, kind),
            pltpu.SemaphoreType.DMA((48,)),
            pltpu.SemaphoreType.DMA((48,)),
        ],
        compiler_params=pltpu.CompilerParams(
            collective_id=7, has_side_effects=True, vmem_limit_bytes=32 * 1024 * 1024
        ),
        name="collect",
    )(oq, vk)


CHUNK = 1024
QUERY_BLOCK = 256
SIDE = (((1,), (1,)), ((), ()))


def attend_kernel(x_ref, y_ref, oq_ref, vk_ref, y_turned, score, slope, total):
    keys = y_ref.shape[0]
    chunks = [slice(start, start + CHUNK) for start in range(0, keys, CHUNK)]
    key_scale = KD ** (-0.5)
    for part in chunks:
        y_turned[:, part] = y_ref[part, :].T
    total[...] = jnp.zeros_like(total)

    def block(index, carry):
        rows = pl.ds(pl.multiple_of(index * QUERY_BLOCK, QUERY_BLOCK), QUERY_BLOCK)
        x_block = x_ref[rows, :]
        wide = x_block.astype(jnp.float32)
        low = lax.broadcasted_iota(jnp.int32, wide.shape, 1) < LOW
        query = jnp.where(low, 0.0, wide).astype(x_block.dtype)
        grad = jnp.where(low, wide, 0.0).astype(x_block.dtype)
        peak = None
        for part in chunks:
            scores = lax.dot_general(y_ref[part, :], query, SIDE, preferred_element_type=jnp.float32)
            score[part, :] = scores
            top = jnp.max(scores, axis=0, keepdims=True)
            peak = top if peak is None else jnp.maximum(peak, top)
        weight = jnp.zeros((1, QUERY_BLOCK), jnp.float32)
        center = jnp.zeros((1, QUERY_BLOCK), jnp.float32)
        for part in chunks:
            grads = lax.dot_general(y_ref[part, :], grad, SIDE, preferred_element_type=jnp.float32)
            slope[part, :] = grads
            terms = jnp.exp2((score[part, :] - peak) * (key_scale * 1.4426950408889634))
            score[part, :] = terms
            weight = weight + jnp.sum(terms, axis=0, keepdims=True)
            center = center + jnp.sum(terms * grads, axis=0, keepdims=True)
        share = 1.0 / weight
        center = center * share
        out = jnp.zeros((WIDE, QUERY_BLOCK), jnp.float32)
        back = jnp.zeros((WIDE, QUERY_BLOCK), jnp.float32)
        low_keys = lax.broadcasted_iota(jnp.int32, (CHUNK, WIDE), 1) < LOW
        for part in chunks:
            probs = score[part, :] * share
            prob_low = probs.astype(jnp.bfloat16)
            grads = (probs * (slope[part, :] - center) * key_scale).astype(jnp.bfloat16)
            out = out + jnp.dot(y_turned[:, part], prob_low, preferred_element_type=jnp.float32)
            back = back + jnp.dot(y_turned[:, part], grads, preferred_element_type=jnp.float32)
            for_values = jnp.dot(prob_low, x_block, preferred_element_type=jnp.float32)
            for_keys = jnp.dot(grads, x_block, preferred_element_type=jnp.float32)
            total[part, :] += jnp.where(low_keys, for_values, for_keys)
        low_rows = lax.broadcasted_iota(jnp.int32, out.shape, 0) < LOW
        oq_ref[rows, :] = jnp.where(low_rows, out, back).T.astype(oq_ref.dtype)
        return carry

    lax.fori_loop(0, x_ref.shape[0] // QUERY_BLOCK, block, 0)
    vk_ref[...] = total[...].astype(vk_ref.dtype)


def attend(x_rows, y_rows):
    vmem = pl.BlockSpec(memory_space=pltpu.VMEM)
    queries, keys = x_rows.shape[0], y_rows.shape[0]
    return pl.pallas_call(
        attend_kernel,
        out_shape=[
            jax.ShapeDtypeStruct(x_rows.shape, x_rows.dtype),
            jax.ShapeDtypeStruct(y_rows.shape, y_rows.dtype),
        ],
        in_specs=[vmem] * 2,
        out_specs=[vmem] * 2,
        scratch_shapes=[
            pltpu.VMEM((WIDE, keys), y_rows.dtype),
            pltpu.VMEM((keys, QUERY_BLOCK), jnp.float32),
            pltpu.VMEM((keys, QUERY_BLOCK), jnp.float32),
            pltpu.VMEM((keys, WIDE), jnp.float32),
        ],
        compiler_params=pltpu.CompilerParams(vmem_limit_bytes=52 * 1024 * 1024),
        name="attend",
        cost_estimate=pl.CostEstimate(
            flops=12 * queries * keys * WIDE, bytes_accessed=8 * keys * WIDE, transcendentals=queries * keys
        ),
    )(x_rows, y_rows)


def padded(block, sides, width):
    for axis, dim in sides:
        count = lax.axis_size(axis)
        forward = [(i, i + 1) for i in range(count - 1)]
        backward = [(target, source) for source, target in forward]
        low = lax.ppermute(
            lax.slice_in_dim(block, block.shape[dim] - width, None, axis=dim), axis, forward
        )
        high = lax.ppermute(lax.slice_in_dim(block, 0, width, axis=dim), axis, backward)
        block = jnp.concatenate([low, block, high], axis=dim)
    return block


def gelu_value(values):
    cubic = GELU_C * (values + 0.044715 * values * values * values)
    return 0.5 * values * (1.0 + jnp.tanh(cubic))


def gelu_slope(values):
    tangent = jnp.tanh(GELU_C * (values + 0.044715 * values * values * values))
    return 0.5 * (1.0 + tangent) + 0.5 * values * (1.0 - tangent * tangent) * GELU_C * (
        1.0 + 3.0 * 0.044715 * values * values
    )


def rounded(values):
    return lax.optimization_barrier(values.astype(jnp.bfloat16)).astype(jnp.float32)


def conv_taps(padded_input, weight, local_bins, mid_width):
    outputs = [
        jnp.einsum(
            "wbc,cm->wbm",
            padded_input[
                :, kernel_tap_index * DILATION_STEP : kernel_tap_index * DILATION_STEP + local_bins
            ],
            weight[:, kernel_tap_index * mid_width : (kernel_tap_index + 1) * mid_width],
            preferred_element_type=jnp.float32,
        )
        for kernel_tap_index in range(3)
    ]
    return outputs[0] + outputs[1] + outputs[2]


def conv_back(padded_gradient, weight, local_bins, mid_width):
    outputs = [
        jnp.einsum(
            "wbm,cm->wbc",
            padded_gradient[
                :,
                (2 - kernel_tap_index) * DILATION_STEP : (2 - kernel_tap_index) * DILATION_STEP
                + local_bins,
            ],
            weight[:, kernel_tap_index * mid_width : (kernel_tap_index + 1) * mid_width],
            preferred_element_type=jnp.float32,
        )
        for kernel_tap_index in range(3)
    ]
    return outputs[0] + outputs[1] + outputs[2]


def on_device(
    inputs,
    conv_weight,
    mix_weight,
    first_gain,
    first_bias,
    second_gain,
    second_bias,
    norm_gain,
    query_weight,
    key_weight,
    value_weight,
    out_weight,
    cotangent,
):
    windows_here, local_bins, model_width = inputs.shape
    devices = lax.axis_size("seq")
    local_count = windows_here * local_bins
    total_rows = local_count * devices * lax.axis_size("batch")
    mid_width = mix_weight.shape[0] * devices
    inputs_flat = inputs.astype(jnp.float32).reshape(local_count, model_width)
    conv_full, mix_full = gather_weights(conv_weight, mix_weight)
    sum_one, square_one = all_sum(
        (jnp.sum(inputs_flat, axis=0), jnp.sum(inputs_flat * inputs_flat, axis=0)), 2
    )
    mean_one = sum_one / total_rows
    scale_one = lax.rsqrt(square_one / total_rows - mean_one * mean_one + EPS)
    hat_one = (inputs_flat - mean_one) * scale_one
    pre_one = hat_one * first_gain + first_bias
    first_activation = (
        gelu_value(pre_one).astype(jnp.bfloat16).reshape(windows_here, local_bins, model_width)
    )
    padded_input = padded(first_activation, (("seq", 1),), DILATION_STEP)
    hidden = conv_taps(padded_input, conv_full, local_bins, mid_width)
    hidden = hidden.reshape(local_count, mid_width)
    sum_two, square_two = all_sum(
        (jnp.sum(hidden, axis=0), jnp.sum(hidden * hidden, axis=0)), 3
    )
    mean_two = sum_two / total_rows
    scale_two = lax.rsqrt(square_two / total_rows - mean_two * mean_two + EPS)
    hat_two = (hidden - mean_two) * scale_two
    pre_two = hat_two * second_gain + second_bias
    act_two = gelu_value(pre_two).astype(jnp.bfloat16)
    mixed_rows = inputs_flat + jnp.dot(act_two, mix_full, preferred_element_type=jnp.float32)
    trunk_rows = rounded(mixed_rows)
    row_mean = jnp.mean(trunk_rows, axis=-1, keepdims=True)
    centered = trunk_rows - row_mean
    row_scale = lax.rsqrt(jnp.mean(centered * centered, axis=-1, keepdims=True) + EPS)
    row_hat = centered * row_scale
    normed = (row_hat * norm_gain).astype(jnp.bfloat16)
    queries = jnp.dot(normed, query_weight, preferred_element_type=jnp.float32).astype(jnp.bfloat16)
    keys_local = jnp.dot(normed, key_weight, preferred_element_type=jnp.float32).astype(
        jnp.bfloat16
    )
    values_local = jnp.dot(normed, value_weight, preferred_element_type=jnp.float32).astype(
        jnp.bfloat16
    )
    cot_flat = cotangent.reshape(local_count, model_width)
    grad_out = jnp.dot(cot_flat, out_weight.T, preferred_element_type=jnp.float32).astype(
        jnp.bfloat16
    )
    x_got, y_got = spread(queries, keys_local, values_local, grad_out)
    oq, vk = attend(x_got.reshape(-1, WIDE), y_got.reshape(-1, WIDE))
    attended_rows, grad_query_rows, grad_value_rows, grad_key_rows = collect(
        oq.reshape(x_got.shape), vk.reshape(y_got.shape)
    )
    encoded = (
        (trunk_rows + jnp.dot(attended_rows, out_weight, preferred_element_type=jnp.float32))
        .astype(jnp.bfloat16)
        .reshape(windows_here, local_bins, model_width)
    )
    grad_normed = jnp.dot(grad_query_rows, query_weight.T, preferred_element_type=jnp.float32)
    grad_normed = grad_normed + jnp.dot(
        grad_key_rows, key_weight.T, preferred_element_type=jnp.float32
    )
    grad_normed = grad_normed + jnp.dot(
        grad_value_rows, value_weight.T, preferred_element_type=jnp.float32
    )
    norm_gain_part = jnp.sum(grad_normed * row_hat, axis=0)
    grad_hat = grad_normed * norm_gain
    grad_trunk = row_scale * (
        grad_hat
        - jnp.mean(grad_hat, axis=-1, keepdims=True)
        - row_hat * jnp.mean(grad_hat * row_hat, axis=-1, keepdims=True)
    )
    grad_mixed = cot_flat.astype(jnp.float32) + grad_trunk
    grad_low = grad_mixed.astype(jnp.bfloat16)
    grad_act_two = jnp.dot(grad_low, mix_full.T, preferred_element_type=jnp.float32)
    grad_pre_two = grad_act_two * gelu_slope(pre_two)
    grad_second_bias, grad_second_gain = all_sum(
        (jnp.sum(grad_pre_two, axis=0), jnp.sum(grad_pre_two * hat_two, axis=0)), 4
    )
    hidden_gradient = (
        (
            second_gain
            * scale_two
            * (
                grad_pre_two
                - grad_second_bias / total_rows
                - hat_two * grad_second_gain / total_rows
            )
        )
        .astype(jnp.bfloat16)
        .reshape(windows_here, local_bins, mid_width)
    )
    padded_gradient = padded(hidden_gradient, (("seq", 1),), DILATION_STEP)
    grad_act_one = conv_back(padded_gradient, conv_full, local_bins, mid_width)
    grad_act_one = grad_act_one.reshape(local_count, model_width)
    grad_pre_one = grad_act_one * gelu_slope(pre_one)
    grad_first_bias, grad_first_gain, grad_norm_gain = all_sum(
        (jnp.sum(grad_pre_one, axis=0), jnp.sum(grad_pre_one * hat_one, axis=0), norm_gain_part), 5
    )
    grad_rows = (
        first_gain
        * scale_one
        * (grad_pre_one - grad_first_bias / total_rows - hat_one * grad_first_gain / total_rows)
    )
    grad_inputs = (
        (grad_mixed + grad_rows).astype(jnp.bfloat16).reshape(windows_here, local_bins, model_width)
    )
    return (
        encoded,
        grad_inputs,
        grad_first_gain,
        grad_first_bias,
        grad_second_gain,
        grad_second_bias,
        grad_norm_gain,
    )


def solution(mesh):
    in_specs = (
        P("batch", "seq", None),
        P("seq", None),
        P("seq", None),
        P(),
        P(),
        P(),
        P(),
        P(),
        P(),
        P(),
        P(),
        P(),
        P("batch", "seq", None),
    )
    out_specs = (P("batch", "seq", None), P("batch", "seq", None), P(), P(), P(), P(), P())
    return jax.shard_map(
        on_device, mesh=mesh, in_specs=in_specs, out_specs=out_specs, check_vma=False
    )
```

profile of v0, /device:TPU:1, one launch (start us, length us, event | category | flops | bytes accessed | tf_op | source)
XLA Modules:
  0.0 278.5 jit_solution(11278573626578324194)
XLA Ops:
  0.6 1.2 convert_reduce_fusion.1
  2.5 18.3 %all_sum_2.1 = f32[24,128]{1,0:T(8,128)} custom-call(f32[24,128]{1,0:T(8,128)} %pad_maximum_fusion.8.x_ref), custom_call_target="tpu_custom_call" | custom-call | tf_op jit(solution)/shard_map/all_sum_2/pallas_call | solution.py:94
  22.3 1.4 multiply_convert_fusion
  23.7 3.2 %collective-permute-start.1 = (bf16[2,16,1536]{2,1,0:T(8,128)(2,1)S(1)}, bf16[2,16,1536]{2,1,0:T(8,128)(2,1)S(1)}, u32[]{:S(2)}, u32[]{:S(2)}) collective-permute-start(bf16[2,16,1536]{2,1,0:T(8,128)(2,1)S(1)} %get-tuple-element.43), channel_id=1, source_target_pairs={{2,0},{4,2},{6,4},{8,6},{10,8},{12,10},{14,12},{16,14},{18,16},{20... | collective-permute-start | bytes 294920 | tf_op jit(solution)/shard_map/ppermute | solution.py:563
  27.0 2.3 collective-permute-start
  29.3 56.6 %gather_weights.1 = (bf16[4,4,2,2,24,2304]{5,4,3,2,1,0:T(8,128)(2,1)}, bf16[4,4,2,2,12,1536]{5,4,3,2,1,0:T(8,128)(2,1)}) custom-call(bf16[24,2304]{1,0:T(8,128)(2,1)} %conv_ref.1, bf16[12,1536]{1,0:T(8,128)(2,1)} %mix_ref.1), custom_call_target="tpu_custom_call" | custom-call | tf_op jit(solution)/shard_map/gather_weights/pallas_call | solution.py:210
  85.9 4.1 %convolution_convert_fusion.g_ref = bf16[128,1536]{1,0:T(8,128)(2,1)S(1)} fusion(bf16[128,1536]{1,0:T(8,128)(2,1)} %bitcast.124, bf16[1536,1536]{1,0:T(8,128)(2,1)} %param.24), kind=kOutput, calls=%fused_computation.7 | convolution fusion | flops 604176384 | bytes 5505024 | tf_op jit(solution)/shard_map/dot_general | solution.py:674
  90.0 2.9 %fusion.6 = f32[2,64,768]{2,1,0:T(8,128)} fusion(bf16[2,64,1536]{2,1,0:T(8,128)(2,1)S(1)} %multiply_convert_fusion, bf16[1536,2304]{1,0:T(8,128)(2,1)} %bitcast.129), kind=kOutput, calls=%fused_computation.15 | convolution fusion | flops 301989888 | bytes 3145728 | tf_op jit(solution)/shard_map/wbc,cm->wbm/dot_general | solution.py:586
  92.9 4.9 %reshape.242 = bf16[768,1536]{1,0:T(8,128)(2,1)} reshape(bf16[4,4,2,2,12,1536]{5,4,3,2,1,0:T(8,128)(2,1)} %get-tuple-element.18) | data formatting | bytes 4718592 | tf_op jit(solution)/shard_map/reshape | solution.py:228
  97.8 2.2 fusion.8
  100.1 2.4 fusion.74
  103.2 12.2 %all_sum_3.1 = f32[16,128]{1,0:T(8,128)} custom-call(f32[16,128]{1,0:T(8,128)} %select_maximum_fusion.3.x_ref), custom_call_target="tpu_custom_call" | custom-call | tf_op jit(solution)/shard_map/all_sum_3/pallas_call | solution.py:94
  117.1 2.3 fusion.2
  121.6 29.0 %spread.1 = (bf16[16,64,256]{2,1,0:T(8,128)(2,1)S(1)}, bf16[2,2,16,64,256]{4,3,2,1,0:T(8,128)(2,1)S(1)}) custom-call(bf16[128,512]{1,0:T(8,128)(2,1)S(1)} %convolution_convert_fusion.3.q_ref, bf16[128,512]{1,0:T(8,128)(2,1)S(1)} %convolution_convert_fusion.2.k_ref, bf16[128,1536]{1,0:T(8,128)(2,1)S(1)} %convolution_convert_fusion.1.v_ref, ...), custom_call_target="tpu_custom_call" | custom-call | tf_op jit(solution)/shard_map/spread/pallas_call | solution.py:336
  150.6 1.3 copy-done.2
  151.9 24.6 %attend.1 = (bf16[1024,256]{1,0:T(8,128)(2,1)S(1)}, bf16[4096,256]{1,0:T(8,128)(2,1)}) custom-call(bf16[1024,256]{1,0:T(8,128)(2,1)S(1)} %bitcast.120, bf16[4096,256]{1,0:T(8,128)(2,1)} %bitcast.119), custom_call_target="tpu_custom_call" | custom-call | flops 12884901888 | bytes 8388608 | tf_op jit(solution)/shard_map/attend/pallas_call | solution.py:533
  176.6 1.6 copy-done.1
  178.2 32.7 %collect.1 = (bf16[128,1536]{1,0:T(8,128)(2,1)S(1)}, bf16[128,512]{1,0:T(8,128)(2,1)S(1)}, bf16[128,1536]{1,0:T(8,128)(2,1)S(1)}, bf16[128,512]{1,0:T(8,128)(2,1)S(1)}) custom-call(bf16[16,64,256]{2,1,0:T(8,128)(2,1)S(1)} %bitcast.118, bf16[2,2,16,64,256]{4,3,2,1,0:T(8,128)(2,1)S(1)} %bitcast.117), custom_call_target="tpu_custom_call" | custom-call | tf_op jit(solution)/shard_map/collect/pallas_call | solution.py:446
  210.9 1.6 fusion.78
  215.0 1.8 fusion.73
  217.4 15.6 %all_sum_4.1 = f32[16,128]{1,0:T(8,128)} custom-call(f32[16,128]{1,0:T(8,128)} %select_maximum_fusion.2.x_ref), custom_call_target="tpu_custom_call" | custom-call | tf_op jit(solution)/shard_map/all_sum_4/pallas_call | solution.py:94
  233.7 1.3 broadcast_multiply_fusion.1
  235.0 3.9 %fusion.3 = bf16[128,1536]{1,0:T(8,128)(2,1)} fusion(bf16[128,1536]{1,0:T(8,128)(2,1)S(1)} %get-tuple-element.23, bf16[1536,1536]{1,0:T(8,128)(2,1)} %param.24, bf16[128,1536]{1,0:T(8,128)(2,1)S(1)} %fusion.2), kind=kOutput, calls=%fused_computation.9 | convolution fusion | flops 604569600 | bytes 5898240 | tf_op jit(solution)/shard_map/dot_general | solution.py:683
  239.0 3.1 %collective-permute-start.3 = (bf16[2,16,768]{2,1,0:T(8,128)(2,1)S(1)}, bf16[2,16,768]{2,1,0:T(8,128)(2,1)S(1)}, u32[]{:S(2)}, u32[]{:S(2)}) collective-permute-start(bf16[2,16,768]{2,1,0:T(8,128)(2,1)S(1)} %get-tuple-element.45), channel_id=1, source_target_pairs={{0,2},{2,4},{4,6},{6,8},{8,10},{10,12},{12,14},{14,16},{16,18},{18... | collective-permute-start | bytes 147464 | tf_op jit(solution)/shard_map/ppermute | solution.py:560
  242.2 2.6 fusion.5
  244.8 1.9 collective-permute-start.2
  246.7 2.5 fusion.7
  250.2 3.9 %fusion.72 = (f32[1536]{0:T(1024)S(1)}, f32[1536]{0:T(1024)S(1)}, f32[2,64,1536]{2,1,0:T(8,128)}) fusion(f32[1536]{0:T(1024)S(1)} %get-tuple-element.49, f32[1536]{0:T(1024)S(1)} %multiply_bitcast_fusion, bf16[2,64,1536]{2,1,0:T(8,128)(2,1)S(1)} %copy-done.4, f32[1536]{0:T(1024)S(1)} %copy-done.15, f32[1536]{0:T(1024)S(1)} %copy-done.14, ...), kind=kOutput, calls=%fused_computation.130 | convolution fusion | flops 307885056 | bytes 5394432 | tf_op jit(solution)/shard_map/wbm,cm->wbc/dot_general | solution.py:601
  254.7 18.4 %all_sum_5.1 = f32[40,128]{1,0:T(8,128)} custom-call(f32[40,128]{1,0:T(8,128)} %select_maximum_fusion.x_ref), custom_call_target="tpu_custom_call" | custom-call | tf_op jit(solution)/shard_map/all_sum_5/pallas_call | solution.py:94
  273.1 1.4 slice_bitcast_fusion.13
  274.5 1.3 broadcast_multiply_fusion
  275.8 2.7 fusion.36
  (74 shorter events, 12.0 us)
Async XLA Ops:
  0.6 119.6 %copy-start = (bf16[1536,512]{1,0:T(8,128)(2,1)S(1)}, bf16[1536,512]{1,0:T(8,128)(2,1)}, u32[]{:S(2)}) copy-start(bf16[1536,512]{1,0:T(8,128)(2,1)} %param.22) | copy-start | bytes 4718596
  23.7 74.1 %copy-start.11 = (bf16[2,64,1536]{2,1,0:T(8,128)(2,1)}, bf16[2,64,1536]{2,1,0:T(8,128)(2,1)S(1)}, u32[]{:S(2)}) copy-start(bf16[2,64,1536]{2,1,0:T(8,128)(2,1)S(1)} %multiply_convert_fusion) | copy-start | bytes 1179652
  23.7 74.1 %collective-permute-start.1 = (bf16[2,16,1536]{2,1,0:T(8,128)(2,1)S(1)}, bf16[2,16,1536]{2,1,0:T(8,128)(2,1)S(1)}, u32[]{:S(2)}, u32[]{:S(2)}) collective-permute-start(bf16[2,16,1536]{2,1,0:T(8,128)(2,1)S(1)} %get-tuple-element.43), channel_id=1, source_target_pairs={{2,0},{4,2},{6,4},{8,6},{10,8},{12,10},{14,12},{16,14},{18,16},{20... | collective-permute-start | bytes 294920 | tf_op jit(solution)/shard_map/ppermute | solution.py:563
  27.0 73.1 %collective-permute-start = (bf16[2,16,1536]{2,1,0:T(8,128)(2,1)S(1)}, bf16[2,16,1536]{2,1,0:T(8,128)(2,1)S(1)}, u32[]{:S(2)}, u32[]{:S(2)}) collective-permute-start(bf16[2,16,1536]{2,1,0:T(8,128)(2,1)S(1)} %get-tuple-element.42), channel_id=1, source_target_pairs={{0,2},{2,4},{4,6},{6,8},{8,10},{10,12},{12,14},{14,16},{16,18},{18... | collective-permute-start | bytes 294920 | tf_op jit(solution)/shard_map/ppermute | solution.py:560
  97.8 2.3 copy-start.20
  100.0 16.0 %copy-start.17 = (f32[768]{0:T(1024)S(1)}, f32[768]{0:T(1024)}, u32[]{:S(2)}) copy-start(f32[768]{0:T(1024)} %param.18) | copy-start | bytes 9220
  100.1 16.8 %copy-start.19 = (f32[768]{0:T(1024)S(1)}, f32[768]{0:T(1024)}, u32[]{:S(2)}) copy-start(f32[768]{0:T(1024)} %param.19) | copy-start | bytes 9220
  100.1 17.0 %copy-start.4 = (bf16[2,64,1536]{2,1,0:T(8,128)(2,1)S(1)}, bf16[2,64,1536]{2,1,0:T(8,128)(2,1)}, u32[]{:S(2)}) copy-start(bf16[2,64,1536]{2,1,0:T(8,128)(2,1)} %param.13) | copy-start | bytes 1179652
  100.1 20.6 %slice-start = ((s8[4718592]{0:T(1024)(128)(4,1)}), s8[524288]{0:T(1024)(128)(4,1)S(1)}, s32[]{:S(2)}) async-start(s8[4718592]{0:T(1024)(128)(4,1)} %bitcast.121), calls=%async_computation | async-start | bytes 1048576
  102.5 14.6 %copy-start.5 = (f32[2,64,768]{2,1,0:T(8,128)}, f32[2,64,768]{2,1,0:T(8,128)S(1)}, u32[]{:S(2)}) copy-start(f32[2,64,768]{2,1,0:T(8,128)S(1)} %get-tuple-element.52) | copy-start | bytes 1179652
  116.9 3.0 %copy-start.9 = (bf16[1536,512]{1,0:T(8,128)(2,1)S(1)}, bf16[1536,512]{1,0:T(8,128)(2,1)}, u32[]{:S(2)}) copy-start(bf16[1536,512]{1,0:T(8,128)(2,1)} %param.21) | copy-start | bytes 4718596
  116.9 3.0 %copy-start.13 = (f32[1536]{0:T(1024)S(1)}, f32[1536]{0:T(1024)}, u32[]{:S(2)}) copy-start(f32[1536]{0:T(1024)} %param.20) | copy-start | bytes 18436
  117.1 3.6 %slice-start.1 = ((s8[4718592]{0:T(1024)(128)(4,1)}), s8[4194304]{0:T(1024)(128)(4,1)S(1)}, s32[]{:S(2)}) async-start(s8[4718592]{0:T(1024)(128)(4,1)} %bitcast.121), calls=%async_computation.1 | async-start | bytes 8388608
  150.6 1.3 copy-start.2
  176.6 1.6 copy-start.1
  213.2 1.0 copy-start.10
  213.2 1.8 copy-start.3
  213.2 1.8 copy-start.6
  215.0 1.8 copy-start.7
  233.7 5.2 %copy-start.18 = (f32[768]{0:T(1024)}, f32[768]{0:T(1024)S(1)}, u32[]{:S(2)}) copy-start(f32[768]{0:T(1024)S(1)} %slice_bitcast_fusion.16) | copy-start | bytes 9220
  235.0 3.9 %copy-start.12 = (f32[128,768]{1,0:T(8,128)S(1)}, f32[128,768]{1,0:T(8,128)}, u32[]{:S(2)}) copy-start(f32[128,768]{1,0:T(8,128)} %get-tuple-element.54) | copy-start | bytes 1179652
  239.0 7.7 %collective-permute-start.3 = (bf16[2,16,768]{2,1,0:T(8,128)(2,1)S(1)}, bf16[2,16,768]{2,1,0:T(8,128)(2,1)S(1)}, u32[]{:S(2)}, u32[]{:S(2)}) collective-permute-start(bf16[2,16,768]{2,1,0:T(8,128)(2,1)S(1)} %get-tuple-element.45), channel_id=1, source_target_pairs={{0,2},{2,4},{4,6},{6,8},{8,10},{10,12},{12,14},{14,16},{16,18},{18... | collective-permute-start | bytes 147464 | tf_op jit(solution)/shard_map/ppermute | solution.py:560
  244.7 5.4 %copy-start.14 = (f32[1536]{0:T(1024)S(1)}, f32[1536]{0:T(1024)}, u32[]{:S(2)}) copy-start(f32[1536]{0:T(1024)} %param.16) | copy-start | bytes 18436
  244.8 5.4 %copy-start.15 = (f32[1536]{0:T(1024)S(1)}, f32[1536]{0:T(1024)}, u32[]{:S(2)}) copy-start(f32[1536]{0:T(1024)} %param.17) | copy-start | bytes 18436
  244.8 5.4 %collective-permute-start.2 = (bf16[2,16,768]{2,1,0:T(8,128)(2,1)S(1)}, bf16[2,16,768]{2,1,0:T(8,128)(2,1)S(1)}, u32[]{:S(2)}, u32[]{:S(2)}) collective-permute-start(bf16[2,16,768]{2,1,0:T(8,128)(2,1)S(1)} %get-tuple-element.44), channel_id=1, source_target_pairs={{2,0},{4,2},{6,4},{8,6},{10,8},{12,10},{14,12},{16,14},{18,16},{20... | collective-permute-start | bytes 147464 | tf_op jit(solution)/shard_map/ppermute | solution.py:563
  249.3 26.6 %copy-start.8 = (f32[128,1536]{1,0:T(8,128)S(1)}, f32[128,1536]{1,0:T(8,128)}, u32[]{:S(2)}) copy-start(f32[128,1536]{1,0:T(8,128)} %copy-done.7) | copy-start | bytes 2359300
  274.5 4.0 %copy-start.16 = (f32[1536]{0:T(1024)}, f32[1536]{0:T(1024)S(1)}, u32[]{:S(2)}) copy-start(f32[1536]{0:T(1024)S(1)} %get-tuple-element.47) | copy-start | bytes 18436
where the time goes:
time: 280 us; the launch traced here: 278 us
  Pallas kernels  208 us (74%)
  matrix products  33.3 us (12%)
  other arithmetic  14.4 us (5%)
  local copies, waits for them, and re-layouts  10.6 us (4%)
  starting transfers between devices  10.6 us (4%)
    pallas_call x4, Pallas kernels, all_sum(): pl.pallas_call(all_sum_kernel, out_shape=jax.ShapeDtypeStruct((full, 128)...  64.6 us
    pallas_call x1, Pallas kernels, gather_weights(): pl.pallas_call(gather_kernel, out_shape=[jax.ShapeDtypeStruct((4, 4, 2, 2...  56.6 us
    pallas_call x1, Pallas kernels, collect(): pl.pallas_call(collect_kernel, out_shape=[jax.ShapeDtypeStruct((128, H *...  32.7 us
    pallas_call x1, Pallas kernels, spread(): pl.pallas_call(spread_kernel, out_shape=[jax.ShapeDtypeStruct((16, 64, WI...  29 us
    pallas_call x1, Pallas kernels, attend(): pl.pallas_call(attend_kernel, out_shape=[jax.ShapeDtypeStruct(x_rows.shap...  24.6 us
    dot_general x3, matrix products, conv_back(): jnp.einsum('wbm,cm->wbc', padded_gradient[:, (2 - kernel_tap_index) * DIL...  8.99 us
    dot_general x3, matrix products, conv_taps(): jnp.einsum('wbc,cm->wbm', padded_input[:, kernel_tap_index * DILATION_STE...  7.44 us
  transfers between devices with their start and end apart: 4, of which 1 were waited for; matrix products, arithmetic and copies ran while one was open for 7% of the time, Pallas kernels for 20%

commit v1 on v0

v1 whole, which is shorter than its diff:
```python
import jax
import jax.numpy as jnp
from jax import lax
from jax.experimental import pallas as pl
from jax.experimental.pallas import tpu as pltpu
from jax.sharding import PartitionSpec as P

H = 8
KD = 64
VD = 192
DILATION_STEP = 16


EPS = 1e-05
GELU_C = 0.7978845608028654


MESH = pl.DeviceIdType.MESH
ROWS = 128
LINE = 8
PLANE = 16
TAP_PARTS = ((0, 0, 0, 768), (1, 0, 768, 384), (1, 1, 0, 384), (2, 1, 384, 768))


def seq_of(z, y, x, core):
    return ((z * 4 + y) * 2 + x) * 2 + core


def remote(source, target, peer, sems, slot):
    copy = pltpu.make_async_remote_copy(
        src_ref=source,
        dst_ref=target,
        send_sem=sems[0].at[slot],
        recv_sem=sems[1].at[slot],
        device_id=peer,
        device_id_type=MESH,
    )
    copy.start()
    return copy


def line_place():
    return lax.axis_index("batch") * 4 + lax.rem(lax.axis_index("seq"), 4)


def line_peer(step):
    other = lax.rem(line_place() + step, LINE)
    spot = lax.axis_index("seq") // 4
    return {"seq": spot * 4 + lax.rem(other, 4), "batch": other // 4}


def plane_peer(step):
    seq = lax.axis_index("seq")
    return {"seq": lax.rem(seq // 4 + step, PLANE) * 4 + lax.rem(seq, 4)}


def ring_peer(step):
    count = 4 * PLANE
    return {"seq": lax.rem(lax.axis_index("seq") + step + count, count)}


def greet_all():
    barrier = pltpu.get_barrier_semaphore()
    peers = [line_peer(step) for step in range(1, LINE)]
    peers += [plane_peer(step) for step in range(1, PLANE)]
    peers += [ring_peer(1), ring_peer(-1)]
    for peer in peers:
        pl.semaphore_signal(barrier, inc=1, device_id=peer, device_id_type=MESH)
    return barrier, len(peers)


def line_send(line, sems, base):
    place = line.at[line_place()]
    return [remote(place, place, line_peer(step), sems, base + step) for step in range(1, LINE)]


def plane_send(line, plane, arrivals, sems, base):
    for copy in arrivals:
        copy.wait_recv()
    total = line[0]
    for i in range(1, LINE):
        total = total + line[i]
    spot = lax.axis_index("seq") // 4
    plane[spot] = total
    place = plane.at[spot]
    return [
        remote(place, place, plane_peer(step), sems, base + LINE + step) for step in range(1, PLANE)
    ]


def plane_sum(plane, arrivals):
    for copy in arrivals:
        copy.wait_recv()
    total = plane[0]
    for i in range(1, PLANE):
        total = total + plane[i]
    return total


def halo_send(middle, low, high, sems, base):
    return [
        remote(middle.at[:, 48:64, :], low, ring_peer(1), sems, (base, 0)),
        remote(middle.at[:, 0:16, :], high, ring_peer(-1), sems, (base, 1)),
    ]


def halo_fill(padded, low, high, copies):
    seq = lax.axis_index("seq")
    last = lax.axis_size("seq") - 1
    for copy in copies:
        copy.wait_recv()
    low_rows = low[...].astype(jnp.float32)
    high_rows = high[...].astype(jnp.float32)
    padded[:, 0:16, :] = jnp.where(seq == 0, 0.0, low_rows).astype(padded.dtype)
    padded[:, 80:96, :] = jnp.where(seq == last, 0.0, high_rows).astype(padded.dtype)


def tap_rows(padded, start):
    return jnp.concatenate([padded[0, start : start + 64, :], padded[1, start : start + 64, :]], axis=0)


def stacked(rows):
    return jnp.concatenate([jnp.sum(part, axis=0, keepdims=True) for part in rows], axis=0)


def gelu_value(values):
    cubic = GELU_C * (values + 0.044715 * values * values * values)
    return 0.5 * values * (1.0 + jnp.tanh(cubic))


def gelu_slope(values):
    tangent = jnp.tanh(GELU_C * (values + 0.044715 * values * values * values))
    return 0.5 * (1.0 + tangent) + 0.5 * values * (1.0 - tangent * tangent) * GELU_C * (
        1.0 + 3.0 * 0.044715 * values * values
    )


def rounded(values):
    return lax.optimization_barrier(values.astype(jnp.bfloat16)).astype(jnp.float32)


CHUNK = 1024
QUERY_BLOCK = 256
SIDE = (((1,), (1,)), ((), ()))
def front_kernel(
    x_ref, conv_ref, mix_ref, gain_ref, bias_ref, cot_ref, out_weight_ref,
    conv_out, mix_out, hidden_out, stats_one_out, stats_two_out, grad_out,
    line_one, plane_one, line_two, plane_two, conv_other, mix_other, mix_land, middle, padded,
    low, high, weight, sum_send, sum_recv, move_send, move_recv, own_sem
):
    seq = lax.axis_index("seq")
    core = lax.rem(seq, 2)
    x = lax.rem(seq // 2, 2)
    y = lax.rem(seq // 4, 4)
    z = seq // 16
    sums = (sum_send, sum_recv)
    moves = (move_send, move_recv)
    total_rows = ROWS * lax.axis_size("seq") * lax.axis_size("batch")
    barrier, count = greet_all()
    load = pltpu.make_async_copy(out_weight_ref, weight, own_sem)
    load.start()
    values = x_ref[...].astype(jnp.float32)
    line_one[line_place()] = stacked([values, values * values])
    pl.semaphore_wait(barrier, count)

    def first_peer(step):
        return {"seq": seq_of(lax.rem(z + step * x, 4), lax.rem(y + step * (1 - x), 4), x, core)}

    def second_peer(step):
        return {"seq": seq_of(lax.rem(z + step * (1 - x), 4), lax.rem(y + step * x, 4), x, core)}

    def y_peer(step):
        return {"seq": seq_of(z, lax.rem(y + step, 4), x, core)}

    def z_peer(step):
        return {"seq": seq_of(lax.rem(z + step, 4), y, x, core)}

    x_peer = {"seq": seq_of(z, y, 1 - x, core)}
    sibling = {"seq": seq_of(z, y, x, 1 - core)}
    outs = (conv_out, mix_land)
    widths = (conv_ref.shape[1] // 2, mix_ref.shape[1] // 2)
    halves = [pl.ds(pl.multiple_of(core * w, w), w) for w in widths]
    far_halves = [pl.ds(pl.multiple_of((1 - core) * w, w), w) for w in widths]

    def move(kind, where, peer, slot):
        place = outs[kind].at[(core, *where)]
        return remote(place, place, peer, moves, (slot, kind))

    started = line_send(line_one, sums, 0)
    line_started = started
    pair_up = [
        remote(conv_ref.at[:, far_halves[0]], conv_other, sibling, moves, (0, 0)),
        remote(mix_ref.at[:, far_halves[1]], mix_other, sibling, moves, (0, 1)),
    ]
    started = started + pair_up
    for kind, mine, other in ((0, conv_ref, conv_other), (1, mix_ref, mix_other)):
        pair_up[kind].wait_recv()
        out = outs[kind]
        here = mine[:, halves[kind]].astype(jnp.float32)
        there = other[...].astype(jnp.float32)
        upper = jnp.where(core == 0, here, there)
        lower = jnp.where(core == 0, there, here)
        out[core, z, y, x] = jnp.concatenate([upper, lower], axis=0).astype(out.dtype)
    to_x = [move(kind, (z, y, x), x_peer, 1) for kind in range(2)]
    spread_out = []
    for kind in range(2):
        for step in (1, 3):
            spread_out.append(move(kind, (z, y, x), first_peer(step), 1 + step))
    plane_started = plane_send(line_one, plane_one, line_started, sums, 0)
    for copy in to_x:
        copy.wait_recv()
    for kind in range(2):
        for step in (1, 3):
            spread_out.append(move(kind, (z, y, 1 - x), second_peer(step), 4 + step))
    first_block, second_block = spread_out[:4], spread_out[4:]
    for kind, step, back in ((0, 1, 3), (1, 3, 1)):
        first_block[2 * kind + step // 2].wait_recv()
        place = (lax.rem(z + back * x, 4), lax.rem(y + back * (1 - x), 4), x)
        spread_out.append(move(kind, place, first_peer(step), 3))
    total = plane_sum(plane_one, plane_started)
    mean = total[0:1, :] / total_rows
    scale = lax.rsqrt(total[1:2, :] / total_rows - mean * mean + EPS)
    stats_one_out[...] = jnp.concatenate([mean, scale], axis=0)
    pre = (values - mean) * scale * gain_ref[...] + bias_ref[...]
    active = gelu_value(pre).astype(middle.dtype)
    for window in range(2):
        middle[window] = active[window * 64 : window * 64 + 64, :]
        padded[window, 16:80, :] = active[window * 64 : window * 64 + 64, :]
    halos = halo_send(middle, low, high, moves, 19)
    for kind, step, back in ((0, 1, 3), (1, 3, 1)):
        second_block[2 * kind + step // 2].wait_recv()
        place = (lax.rem(z + back * (1 - x), 4), lax.rem(y + back * x, 4), 1 - x)
        spread_out.append(move(kind, place, second_peer(step), 6))
    waited = (first_block[0], first_block[3], second_block[0], second_block[3])
    for copy in spread_out:
        if all(copy is not other for other in waited):
            copy.wait_recv()
    whole = slice(None)
    blocks = [[], []]
    across = [[], []]

    def launch(kind):
        for step in (1, 3):
            blocks[kind].append(move(kind, (z, whole, 0), z_peer(step), 7 + step))
            blocks[kind].append(move(kind, (whole, y, 1), y_peer(step), 10 + step))
        across[kind].append(move(kind, (z, whole, 0), sibling, 14))
        across[kind].append(move(kind, (whole, y, 1), sibling, 15))

    def relay(kind):
        for i, (step, part) in enumerate(((1, slice(0, 2)), (3, slice(2, 4)))):
            from_z, from_y = lax.rem(z + 4 - step, 4), lax.rem(y + 4 - step, 4)
            blocks[kind][2 * i].wait_recv()
            blocks[kind].append(move(kind, (from_z, part, 0), z_peer(step), 9 if i == 0 else 24))
            blocks[kind][2 * i + 1].wait_recv()
            blocks[kind].append(move(kind, (part, from_y, 1), y_peer(step), 12 if i == 0 else 25))
            across[kind].append(move(kind, (from_z, whole, 0), sibling, 15 + step))
            across[kind].append(move(kind, (whole, from_y, 1), sibling, 20 + step))

    def finish(kind):
        blocks[kind][4].wait_recv()
        blocks[kind][6].wait_recv()
        across[kind].append(move(kind, (lax.rem(z + 2, 4), whole, 0), sibling, 17))
        blocks[kind][5].wait_recv()
        blocks[kind][7].wait_recv()
        across[kind].append(move(kind, (whole, lax.rem(y + 2, 4), 1), sibling, 22))

    launch(0)
    load.wait()
    grad_out[...] = lax.dot_general(
        cot_ref[...], weight[...], SIDE, preferred_element_type=jnp.float32
    ).astype(grad_out.dtype)
    halo_fill(padded, low, high, halos)

    relay(0)
    launch(1)
    finish(0)
    for copy in across[0]:
        copy.wait_recv()
    terms = {}
    for tap, half, start, size in TAP_PARTS:
        part = conv_out[half, :, :, :, :, start : start + size].reshape(-1, size)
        terms[tap, half] = jnp.dot(tap_rows(padded, 16 * tap), part, preferred_element_type=jnp.float32)
    middle_tap = jnp.concatenate([terms[1, 0], terms[1, 1]], axis=1)
    hidden = terms[0, 0] + middle_tap + terms[2, 1]
    hidden_out[...] = hidden
    line_two[line_place()] = stacked([hidden, hidden * hidden])
    line_again = line_send(line_two, sums, LINE + PLANE)
    relay(1)
    plane_again = plane_send(line_two, plane_two, line_again, sums, LINE + PLANE)
    finish(1)
    for copy in across[1]:
        copy.wait_recv()
    for i in range(4):
        for j in range(4):
            start = (i * 4 + j) * 48
            for half in range(2):
                pair = [mix_land[half, i, j, k].astype(jnp.float32) for k in range(2)]
                columns = slice(half * widths[1], half * widths[1] + widths[1])
                mix_out[start : start + 48, columns] = jnp.concatenate(pair, axis=0).astype(mix_out.dtype)
    stats_two_out[...] = plane_sum(plane_two, plane_again)
    ended = started + to_x + spread_out + halos + plane_started + line_again + plane_again
    for kind in range(2):
        ended += blocks[kind] + across[kind]
    for copy in ended:
        copy.wait_send()


def front(inputs, conv_weight, mix_weight, gain, bias, cot, out_weight):
    vmem = pl.BlockSpec(memory_space=pltpu.VMEM)
    anywhere = pl.BlockSpec(memory_space=pl.ANY)
    width = inputs.shape[1]
    mid_width = conv_weight.shape[1] // 3
    kind = inputs.dtype
    conv_rows, mix_rows = conv_weight.shape[0], mix_weight.shape[0]
    full, wide = jnp.float32, conv_weight.shape[1]
    sems = 2 * (LINE + PLANE)
    conv_full, *rest = pl.pallas_call(
        front_kernel,
        out_shape=[
            jax.ShapeDtypeStruct((2, 4, 4, 2, 2 * conv_rows, wide // 2), kind),
            jax.ShapeDtypeStruct((64 * mix_rows, width), kind),
            jax.ShapeDtypeStruct((ROWS, mid_width), full),
            jax.ShapeDtypeStruct((2, width), full),
            jax.ShapeDtypeStruct((2, mid_width), full),
            jax.ShapeDtypeStruct((ROWS, out_weight.shape[0]), kind),
        ],
        in_specs=[vmem] * 6 + [anywhere],
        out_specs=[vmem] * 6,
        scratch_shapes=[
            pltpu.VMEM((LINE, 2, width), full),
            pltpu.VMEM((PLANE, 2, width), full),
            pltpu.VMEM((LINE, 2, mid_width), full),
            pltpu.VMEM((PLANE, 2, mid_width), full),
            pltpu.VMEM((conv_rows, wide // 2), kind),
            pltpu.VMEM((mix_rows, width // 2), kind),
            pltpu.VMEM((2, 4, 4, 2, 2 * mix_rows, width // 2), kind),
            pltpu.VMEM((2, 64, width), kind),
            pltpu.VMEM((2, 96, width), kind),
            pltpu.VMEM((2, 16, width), kind),
            pltpu.VMEM((2, 16, width), kind),
            pltpu.VMEM(out_weight.shape, kind),
            pltpu.SemaphoreType.DMA((sems,)),
            pltpu.SemaphoreType.DMA((sems,)),
            pltpu.SemaphoreType.DMA((26, 2)),
            pltpu.SemaphoreType.DMA((26, 2)),
            pltpu.SemaphoreType.DMA,
        ],
        compiler_params=pltpu.CompilerParams(
            collective_id=1, has_side_effects=True, vmem_limit_bytes=48 * 1024 * 1024
        ),
        name="front",
    )(inputs, conv_weight, mix_weight, gain, bias, cot, out_weight)
    return [conv_full.reshape(2, -1, wide // 2)] + rest


def tail_kernel(
    grad_ref, hat_ref, factor_ref, norm_ref, x_ref, stats_ref, gain_ref, bias_ref, mixed_ref, conv_ref,
    out_ref, sums_two_out, sums_one_out,
    line_two, plane_two, line_one, plane_one, middle, padded, low, high, hat_one, slope_one, weight,
    sum_send, sum_recv, move_send, move_recv, own_sem
):
    sums = (sum_send, sum_recv)
    moves = (move_send, move_recv)
    total_rows = ROWS * lax.axis_size("seq") * lax.axis_size("batch")
    barrier, count = greet_all()
    load = pltpu.make_async_copy(conv_ref, weight, own_sem)
    load.start()
    grads = grad_ref[...]
    place = line_place()
    line_two[place, 0:2, :] = stacked([grads, grads * hat_ref[...]])
    line_two[place, 2:4, :] = norm_ref[...]
    pl.semaphore_wait(barrier, count)
    started = line_send(line_two, sums, 0)
    mean, scale = stats_ref[0:1, :], stats_ref[1:2, :]
    hat = (x_ref[...].astype(jnp.float32) - mean) * scale
    hat_one[...] = hat
    plane_started = plane_send(line_two, plane_two, started, sums, 0)
    slope_one[...] = gelu_slope(hat * gain_ref[...] + bias_ref[...])
    total = plane_sum(plane_two, plane_started)
    sums_two_out[...] = total
    hidden_grad = (
        factor_ref[...]
        * (grad_ref[...] - total[0:1, :] / total_rows - hat_ref[...] * total[1:2, :] / total_rows)
    ).astype(middle.dtype)
    for window in range(2):
        middle[window] = hidden_grad[window * 64 : window * 64 + 64, :]
        padded[window, 16:80, :] = hidden_grad[window * 64 : window * 64 + 64, :]
    halos = halo_send(middle, low, high, moves, 0)
    load.wait()
    grad_act = None
    for tap, half, start, size in (TAP_PARTS[1], TAP_PARTS[2], TAP_PARTS[0], TAP_PARTS[3]):
        if tap == 0:
            halo_fill(padded, low, high, halos)
        first = 0 if half == 0 or tap == 2 else 384
        term = lax.dot_general(
            tap_rows(padded, 16 * (2 - tap))[:, first : first + size],
            weight[half, :, start : start + size],
            SIDE,
            preferred_element_type=jnp.float32,
        )
        grad_act = term if grad_act is None else grad_act + term
    grad_pre = grad_act * slope_one[...]
    line_one[place] = stacked([grad_pre, grad_pre * hat_one[...]])
    line_again = line_send(line_one, sums, LINE + PLANE)
    plane_again = plane_send(line_one, plane_one, line_again, sums, LINE + PLANE)
    total = plane_sum(plane_one, plane_again)
    sums_one_out[...] = total
    grad_rows = (
        gain_ref[...]
        * scale
        * (grad_pre - total[0:1, :] / total_rows - hat_one[...] * total[1:2, :] / total_rows)
    )
    out_ref[...] = (mixed_ref[...] + grad_rows).astype(out_ref.dtype)
    for copy in started + plane_started + halos + line_again + plane_again:
        copy.wait_send()


def tail(grad_pre, hat_two, factor, norm_part, inputs, stats, gain, bias, mixed, conv_full):
    vmem = pl.BlockSpec(memory_space=pltpu.VMEM)
    anywhere = pl.BlockSpec(memory_space=pl.ANY)
    width, mid_width = inputs.shape[1], grad_pre.shape[1]
    kind, full = inputs.dtype, jnp.float32
    sems = 2 * (LINE + PLANE)
    return pl.pallas_call(
        tail_kernel,
        out_shape=[
            jax.ShapeDtypeStruct((ROWS, width), kind),
            jax.ShapeDtypeStruct((4, mid_width), full),
            jax.ShapeDtypeStruct((2, width), full),
        ],
        in_specs=[vmem] * 9 + [anywhere],
        out_specs=[vmem] * 3,
        scratch_shapes=[
            pltpu.VMEM((LINE, 4, mid_width), full),
            pltpu.VMEM((PLANE, 4, mid_width), full),
            pltpu.VMEM((LINE, 2, width), full),
            pltpu.VMEM((PLANE, 2, width), full),
            pltpu.VMEM((2, 64, mid_width), kind),
            pltpu.VMEM((2, 96, mid_width), kind),
            pltpu.VMEM((2, 16, mid_width), kind),
            pltpu.VMEM((2, 16, mid_width), kind),
            pltpu.VMEM((ROWS, width), full),
            pltpu.VMEM((ROWS, width), full),
            pltpu.VMEM(conv_full.shape, kind),
            pltpu.SemaphoreType.DMA((sems,)),
            pltpu.SemaphoreType.DMA((sems,)),
            pltpu.SemaphoreType.DMA((1, 2)),
            pltpu.SemaphoreType.DMA((1, 2)),
            pltpu.SemaphoreType.DMA,
        ],
        compiler_params=pltpu.CompilerParams(
            collective_id=2, has_side_effects=True, vmem_limit_bytes=40 * 1024 * 1024
        ),
        name="tail",
    )(grad_pre, hat_two, factor, norm_part, inputs, stats, gain, bias, mixed, conv_full)


LOW = VD
WIDE = VD + KD


def spots():
    seq = lax.axis_index("seq")
    core = lax.rem(seq, 2)
    z = seq // 16
    mine = (z // 2) * 8 + lax.rem(seq // 2, 8)
    return seq, core, lax.rem(z + z // 2, 2), mine


def pair_ahead(mine, step):
    return lax.rem(mine // 4 + step // 4, 4) * 4 + lax.rem(lax.rem(mine, 4) + step % 4, 4)


def pair_behind(mine, step):
    return lax.rem(mine // 4 + 4 - step // 4, 4) * 4 + lax.rem(lax.rem(mine, 4) + 4 - step % 4, 4)


def holder(pair, z_low, core):
    upper = pair // 8
    z = upper * 2 + lax.rem(z_low + upper, 2)
    return {"seq": z * 16 + lax.rem(pair, 8) * 2 + core}


def attention_peers(seq, core, z_low, mine):
    z_peer = holder(mine, 1 - z_low, core)
    sibling = {"seq": seq + 1 - 2 * core}
    return z_peer, sibling


def greet(mine, z_low, core, z_peer, sibling):
    barrier = pltpu.get_barrier_semaphore()
    for step in range(1, 16):
        pl.semaphore_signal(
            barrier, inc=1, device_id=holder(pair_ahead(mine, step), z_low, core), device_id_type=MESH
        )
    pl.semaphore_signal(barrier, inc=1, device_id=z_peer, device_id_type=MESH)
    pl.semaphore_signal(barrier, inc=1, device_id=sibling, device_id_type=MESH)
    return barrier


def spread_heads(q_ref, k_ref, v_ref, g_ref, x_out, y_out, x_part, y_part, sems):
    seq, core, z_low, mine = spots()
    z_peer, sibling = attention_peers(seq, core, z_low, mine)
    barrier = greet(mine, z_low, core, z_peer, sibling)
    for window in range(2):
        rows = slice(window * 64, window * 64 + 64)
        for head in range(H):
            pair = window * H + head
            y_part[pair, :, 0:LOW] = v_ref[rows, head * VD : head * VD + VD]
            y_part[pair, :, LOW:WIDE] = k_ref[rows, head * KD : head * KD + KD]
    pl.semaphore_wait(barrier, 17)

    def send(source, target, peer, slot):
        return remote(source, target, peer, sems, slot)

    y_sends = []
    for step in range(1, 16):
        pair = pair_ahead(mine, step)
        peer = holder(pair, z_low, core)
        y_sends.append(send(y_part.at[pair], y_out.at[z_low, core, mine], peer, step))
    for window in range(2):
        rows = slice(window * 64, window * 64 + 64)
        for head in range(H):
            pair = window * H + head
            x_part[pair, :, 0:LOW] = g_ref[rows, head * VD : head * VD + VD]
            x_part[pair, :, LOW:WIDE] = q_ref[rows, head * KD : head * KD + KD]
    x_sends = []
    for step in range(1, 16):
        pair = pair_ahead(mine, step)
        peer = holder(pair, z_low, core)
        x_sends.append(send(x_part.at[pair], x_out.at[mine], peer, 16 + step))
    y_out[z_low, core, mine] = y_part[mine]
    x_out[mine] = x_part[mine]
    along = []
    across = []
    for step in range(16):
        if step > 0:
            y_sends[step - 1].wait_recv()
        place = y_out.at[z_low, core, pair_behind(mine, step)]
        along.append(send(place, place, z_peer, 32 + step))
        across.append(send(place, place, sibling, 48 + step))
    for step in range(16):
        along[step].wait_recv()
        place = y_out.at[1 - z_low, core, pair_behind(mine, step)]
        across.append(send(place, place, sibling, 64 + step))
    for copy in x_sends + across:
        copy.wait_recv()
    for copy in y_sends + x_sends + along + across:
        copy.wait_send()


def collect_heads(
    oq_ref, vk_ref, a_ref, gq_ref, gv_ref, gk_ref, oq_got, vk_got, from_core, to_z, from_z, total, sems
):
    seq, core, z_low, mine = spots()
    z_peer, sibling = attention_peers(seq, core, z_low, mine)

    def send(source, target, peer, slot):
        return remote(source, target, peer, sems, 80 + slot)

    groups = [pl.ds(lax.rem(mine // 4 + k, 4) * 4, 4) for k in range(4)]
    across = []
    for far in range(2):
        z_part = 1 - z_low if far == 0 else z_low
        for k in range(4):
            across.append(
                send(
                    vk_ref.at[z_part, 1 - core, groups[k]],
                    from_core.at[far, groups[k]],
                    sibling,
                    4 * far + k,
                )
            )
    oq_sends = []
    for step in range(1, 16):
        pair = pair_ahead(mine, step)
        oq_sends.append(
            send(oq_ref.at[pair], oq_got.at[mine], holder(pair, z_low, core), 16 + step)
        )
    oq_got[mine] = oq_ref[mine]
    along = []
    for k in range(4):
        across[k].wait_recv()
        summed = vk_ref[1 - z_low, core, groups[k]].astype(jnp.float32) + from_core[
            0, groups[k]
        ].astype(jnp.float32)
        to_z[groups[k]] = summed.astype(to_z.dtype)
        along.append(send(to_z.at[groups[k]], from_z.at[groups[k]], z_peer, 8 + k))
    vk_sends = []
    for k in range(4):
        across[4 + k].wait_recv()
        along[k].wait_recv()
        summed = vk_ref[z_low, core, groups[k]].astype(jnp.float32) + from_core[
            1, groups[k]
        ].astype(jnp.float32)
        summed = summed + from_z[groups[k]].astype(jnp.float32)
        total[groups[k]] = summed.astype(total.dtype)
        for step in range(4 * k, 4 * k + 4):
            if step > 0:
                pair = pair_ahead(mine, step)
                vk_sends.append(
                    send(total.at[pair], vk_got.at[mine], holder(pair, z_low, core), 32 + step)
                )
    vk_got[mine] = total[mine]
    for copy in oq_sends:
        copy.wait_recv()
    for window in range(2):
        rows = slice(window * 64, window * 64 + 64)
        for head in range(H):
            pair = window * H + head
            a_ref[rows, head * VD : head * VD + VD] = oq_got[pair, :, 0:LOW]
            gq_ref[rows, head * KD : head * KD + KD] = oq_got[pair, :, LOW:WIDE]
    for copy in vk_sends:
        copy.wait_recv()
    for window in range(2):
        rows = slice(window * 64, window * 64 + 64)
        for head in range(H):
            pair = window * H + head
            gv_ref[rows, head * VD : head * VD + VD] = vk_got[pair, :, 0:LOW]
            gk_ref[rows, head * KD : head * KD + KD] = vk_got[pair, :, LOW:WIDE]
    for copy in across + oq_sends + along + vk_sends:
        copy.wait_send()


def attend_rows(x_ref, y_ref, oq_ref, vk_ref, y_turned, score, slope, total):
    keys = y_turned.shape[1]
    chunks = [slice(start, start + CHUNK) for start in range(0, keys, CHUNK)]

    def key_rows(part):
        quarter = part.start // CHUNK
        return y_ref[quarter // 2, quarter % 2].reshape(CHUNK, WIDE)

    key_scale = KD ** (-0.5)
    for part in chunks:
        y_turned[:, part] = key_rows(part).T
    total[...] = jnp.zeros_like(total)

    def block(index, carry):
        rows = pl.ds(index * 4, 4)
        x_block = x_ref[rows].reshape(QUERY_BLOCK, WIDE)
        wide = x_block.astype(jnp.float32)
        low = lax.broadcasted_iota(jnp.int32, wide.shape, 1) < LOW
        query = jnp.where(low, 0.0, wide).astype(x_block.dtype)
        grad = jnp.where(low, wide, 0.0).astype(x_block.dtype)
        peak = None
        for part in chunks:
            scores = lax.dot_general(key_rows(part), query, SIDE, preferred_element_type=jnp.float32)
            score[part, :] = scores
            top = jnp.max(scores, axis=0, keepdims=True)
            peak = top if peak is None else jnp.maximum(peak, top)
        weight = jnp.zeros((1, QUERY_BLOCK), jnp.float32)
        center = jnp.zeros((1, QUERY_BLOCK), jnp.float32)
        for part in chunks:
            grads = lax.dot_general(key_rows(part), grad, SIDE, preferred_element_type=jnp.float32)
            slope[part, :] = grads
            terms = jnp.exp2((score[part, :] - peak) * (key_scale * 1.4426950408889634))
            score[part, :] = terms
            weight = weight + jnp.sum(terms, axis=0, keepdims=True)
            center = center + jnp.sum(terms * grads, axis=0, keepdims=True)
        share = 1.0 / weight
        center = center * share
        out = jnp.zeros((WIDE, QUERY_BLOCK), jnp.float32)
        back = jnp.zeros((WIDE, QUERY_BLOCK), jnp.float32)
        low_keys = lax.broadcasted_iota(jnp.int32, (CHUNK, WIDE), 1) < LOW
        for part in chunks:
            probs = score[part, :] * share
            prob_low = probs.astype(jnp.bfloat16)
            grads = (probs * (slope[part, :] - center) * key_scale).astype(jnp.bfloat16)
            out = out + jnp.dot(y_turned[:, part], prob_low, preferred_element_type=jnp.float32)
            back = back + jnp.dot(y_turned[:, part], grads, preferred_element_type=jnp.float32)
            for_values = jnp.dot(prob_low, x_block, preferred_element_type=jnp.float32)
            for_keys = jnp.dot(grads, x_block, preferred_element_type=jnp.float32)
            total[part, :] += jnp.where(low_keys, for_values, for_keys)
        low_rows = lax.broadcasted_iota(jnp.int32, out.shape, 0) < LOW
        turned = jnp.where(low_rows, out, back).T
        oq_ref[rows] = turned.reshape(4, 64, WIDE).astype(oq_ref.dtype)
        return carry

    lax.fori_loop(0, x_ref.shape[0] // 4, block, 0)
    vk_ref[...] = total[...].reshape(vk_ref.shape).astype(vk_ref.dtype)


def attention_kernel(
    q_ref, k_ref, v_ref, g_ref, a_ref, gq_ref, gv_ref, gk_ref,
    x_part, y_part, x_got, y_got, y_turned, score, slope, total, oq, vk,
    oq_got, vk_got, from_core, to_z, from_z, summed, send_sem, recv_sem
):
    sems = (send_sem, recv_sem)
    spread_heads(q_ref, k_ref, v_ref, g_ref, x_got, y_got, x_part, y_part, sems)
    attend_rows(x_got, y_got, oq, vk, y_turned, score, slope, total)
    collect_heads(
        oq, vk, a_ref, gq_ref, gv_ref, gk_ref, oq_got, vk_got, from_core, to_z, from_z, summed, sems
    )


def attention(queries, keys, values, grad_out):
    vmem = pl.BlockSpec(memory_space=pltpu.VMEM)
    kind = queries.dtype
    piece = (16, 64, WIDE)
    count = 4 * 16 * 64
    return pl.pallas_call(
        attention_kernel,
        out_shape=[
            jax.ShapeDtypeStruct((ROWS, H * VD), kind),
            jax.ShapeDtypeStruct((ROWS, H * KD), kind),
            jax.ShapeDtypeStruct((ROWS, H * VD), kind),
            jax.ShapeDtypeStruct((ROWS, H * KD), kind),
        ],
        in_specs=[vmem] * 4,
        out_specs=[vmem] * 4,
        scratch_shapes=[
            pltpu.VMEM(piece, kind),
            pltpu.VMEM(piece, kind),
            pltpu.VMEM(piece, kind),
            pltpu.VMEM((2, 2) + piece, kind),
            pltpu.VMEM((WIDE, count), kind),
            pltpu.VMEM((count, QUERY_BLOCK), jnp.float32),
            pltpu.VMEM((count, QUERY_BLOCK), jnp.float32),
            pltpu.VMEM((count, WIDE), jnp.float32),
            pltpu.VMEM(piece, kind),
            pltpu.VMEM((2, 2) + piece, kind),
            pltpu.VMEM(piece, kind),
            pltpu.VMEM(piece, kind),
            pltpu.VMEM((2,) + piece, kind),
            pltpu.VMEM(piece, kind),
            pltpu.VMEM(piece, kind),
            pltpu.VMEM(piece, kind),
            pltpu.SemaphoreType.DMA((128,)),
            pltpu.SemaphoreType.DMA((128,)),
        ],
        compiler_params=pltpu.CompilerParams(
            collective_id=3, has_side_effects=True, vmem_limit_bytes=56 * 1024 * 1024
        ),
        name="attention",
    )(queries, keys, values, grad_out)


def on_device(
    inputs,
    conv_weight,
    mix_weight,
    first_gain,
    first_bias,
    second_gain,
    second_bias,
    norm_gain,
    query_weight,
    key_weight,
    value_weight,
    out_weight,
    cotangent,
):
    windows_here, local_bins, model_width = inputs.shape
    devices = lax.axis_size("seq")
    local_count = windows_here * local_bins
    total_rows = local_count * devices * lax.axis_size("batch")
    rows_in = inputs.reshape(local_count, model_width)
    inputs_flat = rows_in.astype(jnp.float32)
    cot_flat = cotangent.reshape(local_count, model_width)
    gain_one, bias_one = first_gain[None, :], first_bias[None, :]
    conv_full, mix_full, hidden, stats_one, stats_two, grad_out = front(
        rows_in, conv_weight, mix_weight, gain_one, bias_one, cot_flat, out_weight
    )
    sum_two, square_two = stats_two[0], stats_two[1]
    mean_two = sum_two / total_rows
    scale_two = lax.rsqrt(square_two / total_rows - mean_two * mean_two + EPS)
    hat_two = (hidden - mean_two) * scale_two
    pre_two = hat_two * second_gain + second_bias
    act_two = gelu_value(pre_two).astype(jnp.bfloat16)
    mixed_rows = inputs_flat + jnp.dot(act_two, mix_full, preferred_element_type=jnp.float32)
    trunk_rows = rounded(mixed_rows)
    row_mean = jnp.mean(trunk_rows, axis=-1, keepdims=True)
    centered = trunk_rows - row_mean
    row_scale = lax.rsqrt(jnp.mean(centered * centered, axis=-1, keepdims=True) + EPS)
    row_hat = centered * row_scale
    normed = (row_hat * norm_gain).astype(jnp.bfloat16)
    queries = jnp.dot(normed, query_weight, preferred_element_type=jnp.float32).astype(jnp.bfloat16)
    keys_local = jnp.dot(normed, key_weight, preferred_element_type=jnp.float32).astype(
        jnp.bfloat16
    )
    values_local = jnp.dot(normed, value_weight, preferred_element_type=jnp.float32).astype(
        jnp.bfloat16
    )
    attended_rows, grad_query_rows, grad_value_rows, grad_key_rows = attention(
        queries, keys_local, values_local, grad_out
    )
    encoded = (
        (trunk_rows + jnp.dot(attended_rows, out_weight, preferred_element_type=jnp.float32))
        .astype(jnp.bfloat16)
        .reshape(windows_here, local_bins, model_width)
    )
    grad_normed = jnp.dot(grad_query_rows, query_weight.T, preferred_element_type=jnp.float32)
    grad_normed = grad_normed + jnp.dot(
        grad_key_rows, key_weight.T, preferred_element_type=jnp.float32
    )
    grad_normed = grad_normed + jnp.dot(
        grad_value_rows, value_weight.T, preferred_element_type=jnp.float32
    )
    norm_gain_part = jnp.sum(grad_normed * row_hat, axis=0)
    grad_hat = grad_normed * norm_gain
    grad_trunk = row_scale * (
        grad_hat
        - jnp.mean(grad_hat, axis=-1, keepdims=True)
        - row_hat * jnp.mean(grad_hat * row_hat, axis=-1, keepdims=True)
    )
    grad_mixed = cot_flat.astype(jnp.float32) + grad_trunk
    grad_low = grad_mixed.astype(jnp.bfloat16)
    grad_act_two = jnp.dot(grad_low, mix_full.T, preferred_element_type=jnp.float32)
    grad_pre_two = grad_act_two * gelu_slope(pre_two)
    grad_rows, sums_two, sums_one = tail(
        grad_pre_two,
        hat_two,
        (second_gain * scale_two)[None, :],
        norm_gain_part.reshape(2, -1),
        rows_in,
        stats_one,
        gain_one,
        bias_one,
        grad_mixed,
        conv_full,
    )
    grad_inputs = grad_rows.reshape(windows_here, local_bins, model_width)
    grad_second_bias, grad_second_gain = sums_two[0], sums_two[1]
    grad_norm_gain = sums_two[2:4].reshape(-1)
    grad_first_bias, grad_first_gain = sums_one[0], sums_one[1]
    return (
        encoded,
        grad_inputs,
        grad_first_gain,
        grad_first_bias,
        grad_second_gain,
        grad_second_bias,
        grad_norm_gain,
    )


def solution(mesh):
    in_specs = (
        P("batch", "seq", None),
        P("seq", None),
        P("seq", None),
        P(),
        P(),
        P(),
        P(),
        P(),
        P(),
        P(),
        P(),
        P(),
        P("batch", "seq", None),
    )
    out_specs = (P("batch", "seq", None), P("batch", "seq", None), P(), P(), P(), P(), P())
    return jax.shard_map(
        on_device, mesh=mesh, in_specs=in_specs, out_specs=out_specs, check_vma=False
    )
```

time: 280 us -> 187 us (0.67)
  Pallas kernels: 208 us -> 152 us
  matrix products: 33.3 us -> 15.3 us
  other arithmetic: 14.4 us -> 0.86 us
  starting transfers between devices: 10.6 us -> 0 us
  local copies, waits for them, and re-layouts: 10.6 us -> 17.3 us
    pallas_call x8 -> x3, Pallas kernels: 208 us -> 152 us  [the longest x1 64.2 us: attention(): pl.pallas_call(attention_kernel, out_shape=[jax.ShapeDtypeStruct((ROWS, H...]
    dot_general x7 -> x0, matrix products: 20.5 us -> none  [the longest x3 8.99 us: conv_back(): jnp.einsum('wbm,cm->wbc', padded_gradient[:, (2 - kernel_tap_index) * DIL...]
    ppermute x4 -> x0, starting transfers between devices: 10.6 us -> none  [the longest x2 5.46 us: padded(): lax.ppermute(lax.slice_in_dim(block, block.shape[dim] - width, None, axis...]
    unnamed x46 -> x47, local copies, waits for them, and re-layouts: 3.56 us -> 12 us
    convert_element_type x4 -> x0, other arithmetic: 4.34 us -> none  [the longest x1 2.66 us: on_device(): (grad_mixed + grad_rows).astype(jnp.bfloat16)]
    div x3 -> x0, other arithmetic: 3.28 us -> none  [the longest x1 1.3 us: on_device(): grad_first_bias / total_rows]
    reshape x1 -> x2, local copies, waits for them, and re-layouts: 4.91 us -> 1.91 us  [the longest x1 1.3 us: on_device(): norm_gain_part.reshape(2, -1)]
  transfers between devices with their start and end apart: 4 -> 0, of which waited for: 1 -> 0; matrix products, arithmetic and copies ran while one was open for 7% -> 0% of each run, Pallas kernels for 20% -> 0%
where the time goes in v1:
time: 187 us
  Pallas kernels  152 us (81%)
  local copies, waits for them, and re-layouts  17.3 us (9%)
  matrix products  15.3 us (8%)
    pallas_call x1, Pallas kernels, attention(): pl.pallas_call(attention_kernel, out_shape=[jax.ShapeDtypeStruct((ROWS, H...  64.2 us
    pallas_call x1, Pallas kernels, front(): pl.pallas_call(front_kernel, out_shape=[jax.ShapeDtypeStruct((2, 4, 4, 2,...  58.2 us
    pallas_call x1, Pallas kernels, tail(): pl.pallas_call(tail_kernel, out_shape=[jax.ShapeDtypeStruct((ROWS, width)...  29.8 us
    unnamed x47, local copies, waits for them, and re-layouts  12 us
    dot_general x1, matrix products, on_device(): jnp.dot(attended_rows, out_weight, preferred_element_type=jnp.float32)  4.05 us
    dot_general x1, matrix products, on_device(): jnp.dot(grad_value_rows, value_weight.T, preferred_element_type=jnp.float32)  4 us

profile of v1, /device:TPU:1, one launch (start us, length us, event | category | flops | bytes accessed | tf_op | source)
XLA Modules:
  0.0 186.6 jit_solution(17612116802676652347)
XLA Ops:
  0.6 0.8 broadcast_in_dim.6.gain_ref
  1.5 0.7 broadcast_in_dim.7.bias_ref
  2.2 1.0 copy-done.2
  3.2 1.0 copy-done.4
  4.2 0.9 copy-done.8
  5.1 0.8 copy-done.9
  5.9 58.2 %front.1 = (bf16[2,4,4,2,48,1152]{5,4,3,2,1,0:T(8,128)(2,1)}, bf16[768,1536]{1,0:T(8,128)(2,1)S(1)}, f32[128,768]{1,0:T(8,128)S(1)}, f32[2,1536]{1,0:T(2,128)S(1...) custom-call(bf16[128,1536]{1,0:T(8,128)(2,1)S(1)} %bitcast.20, bf16[24,2304]{1,0:T(8,128)(2,1)S(1)} %copy-done.8, ...), custom_call_target="tpu_custom_call" | custom-call | tf_op jit(solution)/shard_map/front/pallas_call | solution.py:317
  64.2 0.5 fusion.1
  64.9 0.3 fusion.15
  65.2 0.5 copy-done.14
  65.7 1.1 convolution_convert_fusion.2.q_ref
  66.7 1.1 convolution_convert_fusion.1.k_ref
  67.9 1.6 convolution_convert_fusion.v_ref
  69.4 64.2 %attention.1 = (bf16[128,1536]{1,0:T(8,128)(2,1)}, bf16[128,512]{1,0:T(8,128)(2,1)}, bf16[128,1536]{1,0:T(8,128)(2,1)}, bf16[128,512]{1,0:T(8,128)(2,1)}) custom-call(bf16[128,512]{1,0:T(8,128)(2,1)} %convolution_convert_fusion.2.q_ref, bf16[128,512]{1,0:T(8,128)(2,1)} %convolution_convert_fusion.1.k_ref, bf16[128,1536]{1,0:T(8,128)(2,1)} %convolution_convert_fusion.v_ref, ...), custom_call_target="tpu_custom_call" | custom-call | tf_op jit(solution)/shard_map/attention/pallas_call | solution.py:701
  133.7 4.1 %fusion.2 = bf16[128,1536]{1,0:T(8,128)(2,1)} fusion(bf16[128,1536]{1,0:T(8,128)(2,1)} %get-tuple-element.24, bf16[1536,1536]{1,0:T(8,128)(2,1)} %out_weight_ref.1, bf16[128,1536]{1,0:T(8,128)(2,1)S(1)} %fusion.1), kind=kOutput, calls=%fused_computation.6 | convolution fusion | flops 604569600 | bytes 5898240 | tf_op jit(solution)/shard_map/dot_general | solution.py:788
  137.7 4.0 %fusion.37 = f32[128,1536]{1,0:T(8,128)S(1)} fusion(bf16[128,1536]{1,0:T(8,128)(2,1)S(1)} %copy-done.15, bf16[1536,1536]{1,0:T(8,128)(2,1)} %param.23), kind=kOutput, calls=%fused_computation.59 | convolution fusion | flops 603979776 | bytes 5898240 | tf_op jit(solution)/shard_map/dot_general | solution.py:796
  141.7 0.6 fusion.36
  142.6 1.4 fusion.14
  144.0 0.4 fusion.13.mixed_ref
  144.4 1.0 convolution_multiply_fusion.grad_ref
  145.4 0.6 broadcast_in_dim.8.factor_ref
  146.0 1.3 reshape.69.norm_ref
  147.3 3.0 %copy-done.1 = bf16[2,4,4,2,48,1152]{5,4,3,2,1,0:T(8,128)(2,1)S(1)} copy-done((bf16[2,4,4,2,48,1152]{5,4,3,2,1,0:T(8,128)(2,1)S(1)}, bf16[2,4,4,2,48,1152]{5,4,3,2,1,0:T(8,128)(2,1)}, u32[]{:S(2)}) %copy-start.1) | copy-done | bytes 7077912
  150.3 0.7 copy-done.10
  151.0 0.7 copy-done.11
  151.7 0.7 copy-done.13
  152.4 29.8 %tail.1 = (bf16[128,1536]{1,0:T(8,128)(2,1)S(1)}, f32[4,768]{1,0:T(4,128)S(1)}, f32[2,1536]{1,0:T(2,128)S(1)}) custom-call(f32[128,768]{1,0:T(8,128)S(1)} %convolution_multiply_fusion.grad_ref, f32[128,768]{1,0:T(8,128)S(1)} %subtract_multiply_fusion.hat_ref, f32[1,768]{1,0:T(1,128)S(1)} %copy-done.11, f32[2,768]{1,0:T(2,128)S(1)} %copy-done.10, ...), custom_call_target="tpu_custom_call" | custom-call | tf_op jit(solution)/shard_map/tail/pallas_call | solution.py:424
  182.2 0.7 copy-done.6
  183.0 0.6 slice_reduce_fusion
  183.6 0.6 slice_reduce_fusion.2
  184.2 0.6 reshape.72
  184.8 1.8 copy.21
  (45 shorter events, 0.5 us)
Async XLA Ops:
  0.6 66.1 %copy-start = (bf16[1536,512]{1,0:T(8,128)(2,1)S(1)}, bf16[1536,512]{1,0:T(8,128)(2,1)}, u32[]{:S(2)}) copy-start(bf16[1536,512]{1,0:T(8,128)(2,1)} %param.22) | copy-start | bytes 4718596
  2.2 1.0 copy-start.2
  3.2 1.0 copy-start.4
  4.2 0.9 copy-start.8
  5.1 0.8 copy-start.9
  5.9 58.3 %copy-start.19 = (f32[768]{0:T(1024)S(1)}, f32[768]{0:T(1024)}, u32[]{:S(2)}) copy-start(f32[768]{0:T(1024)} %param.18) | copy-start | bytes 9220
  5.9 58.3 %copy-start.20 = (f32[768]{0:T(1024)S(1)}, f32[768]{0:T(1024)}, u32[]{:S(2)}) copy-start(f32[768]{0:T(1024)} %param.19) | copy-start | bytes 9220
  5.9 62.0 %slice-start = ((s8[4718592]{0:T(1024)(128)(4,1)}), s8[524288]{0:T(1024)(128)(4,1)S(1)}, s32[]{:S(2)}) async-start(s8[4718592]{0:T(1024)(128)(4,1)} %bitcast.25), calls=%async_computation | async-start | bytes 1048576
  64.1 0.8 copy-start.7
  64.1 0.8 copy-start.12
  64.1 1.5 copy-start.14
  64.1 1.5 copy-start.18
  64.2 3.6 %slice-start.1 = ((s8[4718592]{0:T(1024)(128)(4,1)}), s8[4194304]{0:T(1024)(128)(4,1)S(1)}, s32[]{:S(2)}) async-start(s8[4718592]{0:T(1024)(128)(4,1)} %bitcast.25), calls=%async_computation.1 | async-start | bytes 8388608
  133.6 4.1 %copy-start.15 = (bf16[128,1536]{1,0:T(8,128)(2,1)S(1)}, bf16[128,1536]{1,0:T(8,128)(2,1)}, u32[]{:S(2)}) copy-start(bf16[128,1536]{1,0:T(8,128)(2,1)} %get-tuple-element.27) | copy-start | bytes 1179652
  137.7 4.0 %copy-start.17 = (bf16[128,512]{1,0:T(8,128)(2,1)S(1)}, bf16[128,512]{1,0:T(8,128)(2,1)}, u32[]{:S(2)}) copy-start(bf16[128,512]{1,0:T(8,128)(2,1)} %get-tuple-element.25) | copy-start | bytes 393220
  141.7 0.9 copy-start.16
  142.4 1.6 copy-start.5
  144.4 2.9 %copy-start.3 = (bf16[2,64,1536]{2,1,0:T(8,128)(2,1)S(1)}, bf16[2,64,1536]{2,1,0:T(8,128)(2,1)}, u32[]{:S(2)}) copy-start(bf16[2,64,1536]{2,1,0:T(8,128)(2,1)} %param.13) | copy-start | bytes 1179652
  147.3 3.0 %copy-start.1 = (bf16[2,4,4,2,48,1152]{5,4,3,2,1,0:T(8,128)(2,1)S(1)}, bf16[2,4,4,2,48,1152]{5,4,3,2,1,0:T(8,128)(2,1)}, u32[]{:S(2)}) copy-start(bf16[2,4,4,2,48,1152]{5,4,3,2,1,0:T(8,128)(2,1)} %get-tuple-element.29) | copy-start | bytes 21233668
  150.3 0.7 copy-start.10
  151.0 0.7 copy-start.11
  151.7 0.7 copy-start.13
  182.2 0.7 copy-start.6

commit v2 on v1

--- a/solution.py
+++ b/solution.py
@@ -143,10 +143,10 @@
 QUERY_BLOCK = 256
 SIDE = (((1,), (1,)), ((), ()))
 def front_kernel(
-    x_ref, conv_ref, mix_ref, gain_ref, bias_ref, cot_ref, out_weight_ref,
+    x_from, conv_from, mix_from, gain_ref, bias_ref, cot_from, out_weight_ref,
     conv_out, mix_out, hidden_out, stats_one_out, stats_two_out, grad_out,
     line_one, plane_one, line_two, plane_two, conv_other, mix_other, mix_land, middle, padded,
-    low, high, weight, sum_send, sum_recv, move_send, move_recv, own_sem
+    low, high, weight, x_ref, conv_ref, mix_ref, cot_ref, sum_send, sum_recv, move_send, move_recv, own_sem
 ):
     seq = lax.axis_index("seq")
     core = lax.rem(seq, 2)
@@ -157,8 +157,21 @@
     moves = (move_send, move_recv)
     total_rows = ROWS * lax.axis_size("seq") * lax.axis_size("batch")
     barrier, count = greet_all()
-    load = pltpu.make_async_copy(out_weight_ref, weight, own_sem)
-    load.start()
+    loads = [
+        pltpu.make_async_copy(source, target, own_sem.at[i])
+        for i, (source, target) in enumerate(
+            (
+                (x_from, x_ref),
+                (conv_from, conv_ref),
+                (mix_from, mix_ref),
+                (cot_from, cot_ref),
+                (out_weight_ref, weight),
+            )
+        )
+    ]
+    for load in loads:
+        load.start()
+    loads[0].wait()
     values = x_ref[...].astype(jnp.float32)
     line_one[line_place()] = stacked([values, values * values])
     pl.semaphore_wait(barrier, count)
@@ -189,11 +202,12 @@
     started = line_send(line_one, sums, 0)
     line_started = started
     pair_up = [
-        remote(conv_ref.at[:, far_halves[0]], conv_other, sibling, moves, (0, 0)),
-        remote(mix_ref.at[:, far_halves[1]], mix_other, sibling, moves, (0, 1)),
+        remote(conv_from.at[:, far_halves[0]], conv_other, sibling, moves, (0, 0)),
+        remote(mix_from.at[:, far_halves[1]], mix_other, sibling, moves, (0, 1)),
     ]
     started = started + pair_up
     for kind, mine, other in ((0, conv_ref, conv_other), (1, mix_ref, mix_other)):
+        loads[1 + kind].wait()
         pair_up[kind].wait_recv()
         out = outs[kind]
         here = mine[:, halves[kind]].astype(jnp.float32)
@@ -221,7 +235,7 @@
     mean = total[0:1, :] / total_rows
     scale = lax.rsqrt(total[1:2, :] / total_rows - mean * mean + EPS)
     stats_one_out[...] = jnp.concatenate([mean, scale], axis=0)
-    pre = (values - mean) * scale * gain_ref[...] + bias_ref[...]
+    pre = (values - mean) * scale * gain_ref[...][None, :] + bias_ref[...][None, :]
     active = gelu_value(pre).astype(middle.dtype)
     for window in range(2):
         middle[window] = active[window * 64 : window * 64 + 64, :]
@@ -265,7 +279,8 @@
         across[kind].append(move(kind, (whole, lax.rem(y + 2, 4), 1), sibling, 22))
 
     launch(0)
-    load.wait()
+    loads[3].wait()
+    loads[4].wait()
     grad_out[...] = lax.dot_general(
         cot_ref[...], weight[...], SIDE, preferred_element_type=jnp.float32
     ).astype(grad_out.dtype)
@@ -324,7 +339,7 @@
             jax.ShapeDtypeStruct((2, mid_width), full),
             jax.ShapeDtypeStruct((ROWS, out_weight.shape[0]), kind),
         ],
-        in_specs=[vmem] * 6 + [anywhere],
+        in_specs=[anywhere] * 3 + [vmem] * 2 + [anywhere] * 2,
         out_specs=[vmem] * 6,
         scratch_shapes=[
             pltpu.VMEM((LINE, 2, width), full),
@@ -339,11 +354,15 @@
             pltpu.VMEM((2, 16, width), kind),
             pltpu.VMEM((2, 16, width), kind),
             pltpu.VMEM(out_weight.shape, kind),
+            pltpu.VMEM(inputs.shape, kind),
+            pltpu.VMEM(conv_weight.shape, kind),
+            pltpu.VMEM(mix_weight.shape, kind),
+            pltpu.VMEM(cot.shape, kind),
             pltpu.SemaphoreType.DMA((sems,)),
             pltpu.SemaphoreType.DMA((sems,)),
             pltpu.SemaphoreType.DMA((26, 2)),
             pltpu.SemaphoreType.DMA((26, 2)),
-            pltpu.SemaphoreType.DMA,
+            pltpu.SemaphoreType.DMA((5,)),
         ],
         compiler_params=pltpu.CompilerParams(
             collective_id=1, has_side_effects=True, vmem_limit_bytes=48 * 1024 * 1024
@@ -353,108 +372,6 @@
     return [conv_full.reshape(2, -1, wide // 2)] + rest
 
 
-def tail_kernel(
-    grad_ref, hat_ref, factor_ref, norm_ref, x_ref, stats_ref, gain_ref, bias_ref, mixed_ref, conv_ref,
-    out_ref, sums_two_out, sums_one_out,
-    line_two, plane_two, line_one, plane_one, middle, padded, low, high, hat_one, slope_one, weight,
-    sum_send, sum_recv, move_send, move_recv, own_sem
-):
-    sums = (sum_send, sum_recv)
-    moves = (move_send, move_recv)
-    total_rows = ROWS * lax.axis_size("seq") * lax.axis_size("batch")
-    barrier, count = greet_all()
-    load = pltpu.make_async_copy(conv_ref, weight, own_sem)
-    load.start()
-    grads = grad_ref[...]
-    place = line_place()
-    line_two[place, 0:2, :] = stacked([grads, grads * hat_ref[...]])
-    line_two[place, 2:4, :] = norm_ref[...]
-    pl.semaphore_wait(barrier, count)
-    started = line_send(line_two, sums, 0)
-    mean, scale = stats_ref[0:1, :], stats_ref[1:2, :]
-    hat = (x_ref[...].astype(jnp.float32) - mean) * scale
-    hat_one[...] = hat
-    plane_started = plane_send(line_two, plane_two, started, sums, 0)
-    slope_one[...] = gelu_slope(hat * gain_ref[...] + bias_ref[...])
-    total = plane_sum(plane_two, plane_started)
-    sums_two_out[...] = total
-    hidden_grad = (
-        factor_ref[...]
-        * (grad_ref[...] - total[0:1, :] / total_rows - hat_ref[...] * total[1:2, :] / total_rows)
-    ).astype(middle.dtype)
-    for window in range(2):
-        middle[window] = hidden_grad[window * 64 : window * 64 + 64, :]
-        padded[window, 16:80, :] = hidden_grad[window * 64 : window * 64 + 64, :]
-    halos = halo_send(middle, low, high, moves, 0)
-    load.wait()
-    grad_act = None
-    for tap, half, start, size in (TAP_PARTS[1], TAP_PARTS[2], TAP_PARTS[0], TAP_PARTS[3]):
-        if tap == 0:
-            halo_fill(padded, low, high, halos)
-        first = 0 if half == 0 or tap == 2 else 384
-        term = lax.dot_general(
-            tap_rows(padded, 16 * (2 - tap))[:, first : first + size],
-            weight[half, :, start : start + size],
-            SIDE,
-            preferred_element_type=jnp.float32,
-        )
-        grad_act = term if grad_act is None else grad_act + term
-    grad_pre = grad_act * slope_one[...]
-    line_one[place] = stacked([grad_pre, grad_pre * hat_one[...]])
-    line_again = line_send(line_one, sums, LINE + PLANE)
-    plane_again = plane_send(line_one, plane_one, line_again, sums, LINE + PLANE)
-    total = plane_sum(plane_one, plane_again)
-    sums_one_out[...] = total
-    grad_rows = (
-        gain_ref[...]
-        * scale
-        * (grad_pre - total[0:1, :] / total_rows - hat_one[...] * total[1:2, :] / total_rows)
-    )
-    out_ref[...] = (mixed_ref[...] + grad_rows).astype(out_ref.dtype)
-    for copy in started + plane_started + halos + line_again + plane_again:
-        copy.wait_send()
-
-
-def tail(grad_pre, hat_two, factor, norm_part, inputs, stats, gain, bias, mixed, conv_full):
-    vmem = pl.BlockSpec(memory_space=pltpu.VMEM)
-    anywhere = pl.BlockSpec(memory_space=pl.ANY)
-    width, mid_width = inputs.shape[1], grad_pre.shape[1]
-    kind, full = inputs.dtype, jnp.float32
-    sems = 2 * (LINE + PLANE)
-    return pl.pallas_call(
-        tail_kernel,
-        out_shape=[
-            jax.ShapeDtypeStruct((ROWS, width), kind),
-            jax.ShapeDtypeStruct((4, mid_width), full),
-            jax.ShapeDtypeStruct((2, width), full),
-        ],
-        in_specs=[vmem] * 9 + [anywhere],
-        out_specs=[vmem] * 3,
-        scratch_shapes=[
-            pltpu.VMEM((LINE, 4, mid_width), full),
-            pltpu.VMEM((PLANE, 4, mid_width), full),
-            pltpu.VMEM((LINE, 2, width), full),
-            pltpu.VMEM((PLANE, 2, width), full),
-            pltpu.VMEM((2, 64, mid_width), kind),
-            pltpu.VMEM((2, 96, mid_width), kind),
-            pltpu.VMEM((2, 16, mid_width), kind),
-            pltpu.VMEM((2, 16, mid_width), kind),
-            pltpu.VMEM((ROWS, width), full),
-            pltpu.VMEM((ROWS, width), full),
-            pltpu.VMEM(conv_full.shape, kind),
-            pltpu.SemaphoreType.DMA((sems,)),
-            pltpu.SemaphoreType.DMA((sems,)),
-            pltpu.SemaphoreType.DMA((1, 2)),
-            pltpu.SemaphoreType.DMA((1, 2)),
-            pltpu.SemaphoreType.DMA,
-        ],
-        compiler_params=pltpu.CompilerParams(
-            collective_id=2, has_side_effects=True, vmem_limit_bytes=40 * 1024 * 1024
-        ),
-        name="tail",
-    )(grad_pre, hat_two, factor, norm_part, inputs, stats, gain, bias, mixed, conv_full)
-
-
 LOW = VD
 WIDE = VD + KD
 
@@ -487,28 +404,24 @@
     return z_peer, sibling
 
 
-def greet(mine, z_low, core, z_peer, sibling):
-    barrier = pltpu.get_barrier_semaphore()
-    for step in range(1, 16):
-        pl.semaphore_signal(
-            barrier, inc=1, device_id=holder(pair_ahead(mine, step), z_low, core), device_id_type=MESH
-        )
-    pl.semaphore_signal(barrier, inc=1, device_id=z_peer, device_id_type=MESH)
-    pl.semaphore_signal(barrier, inc=1, device_id=sibling, device_id_type=MESH)
-    return barrier
-
-
-def spread_heads(q_ref, k_ref, v_ref, g_ref, x_out, y_out, x_part, y_part, sems):
+def greet_attention(barrier):
+    seq, core, z_low, mine = spots()
+    peers = [holder(pair_ahead(mine, step), z_low, core) for step in range(1, 16)]
+    peers += attention_peers(seq, core, z_low, mine)
+    for peer in peers:
+        pl.semaphore_signal(barrier, inc=1, device_id=peer, device_id_type=MESH)
+    return len(peers)
+
+
+def spread_heads(q_ref, k_ref, v_ref, g_ref, x_out, y_out, x_part, y_part, sems, meanwhile):
     seq, core, z_low, mine = spots()
     z_peer, sibling = attention_peers(seq, core, z_low, mine)
-    barrier = greet(mine, z_low, core, z_peer, sibling)
     for window in range(2):
         rows = slice(window * 64, window * 64 + 64)
         for head in range(H):
             pair = window * H + head
             y_part[pair, :, 0:LOW] = v_ref[rows, head * VD : head * VD + VD]
             y_part[pair, :, LOW:WIDE] = k_ref[rows, head * KD : head * KD + KD]
-    pl.semaphore_wait(barrier, 17)
 
     def send(source, target, peer, slot):
         return remote(source, target, peer, sems, slot)
@@ -539,6 +452,7 @@
         place = y_out.at[z_low, core, pair_behind(mine, step)]
         along.append(send(place, place, z_peer, 32 + step))
         across.append(send(place, place, sibling, 48 + step))
+    meanwhile()
     for step in range(16):
         along[step].wait_recv()
         place = y_out.at[1 - z_low, core, pair_behind(mine, step)]
@@ -550,7 +464,8 @@
 
 
 def collect_heads(
-    oq_ref, vk_ref, a_ref, gq_ref, gv_ref, gk_ref, oq_got, vk_got, from_core, to_z, from_z, total, sems
+    oq_ref, vk_ref, a_ref, gq_ref, gv_ref, gk_ref, oq_got, vk_got, from_core, to_z, from_z, total, sems,
+    meanwhile
 ):
     seq, core, z_low, mine = spots()
     z_peer, sibling = attention_peers(seq, core, z_low, mine)
@@ -610,6 +525,7 @@
             pair = window * H + head
             a_ref[rows, head * VD : head * VD + VD] = oq_got[pair, :, 0:LOW]
             gq_ref[rows, head * KD : head * KD + KD] = oq_got[pair, :, LOW:WIDE]
+    meanwhile()
     for copy in vk_sends:
         copy.wait_recv()
     for window in range(2):
@@ -680,59 +596,201 @@
     vk_ref[...] = total[...].reshape(vk_ref.shape).astype(vk_ref.dtype)
 
 
-def attention_kernel(
-    q_ref, k_ref, v_ref, g_ref, a_ref, gq_ref, gv_ref, gk_ref,
-    x_part, y_part, x_got, y_got, y_turned, score, slope, total, oq, vk,
-    oq_got, vk_got, from_core, to_z, from_z, summed, send_sem, recv_sem
+def back_kernel(
+    x_ref, hidden_ref, stats_one_ref, stats_two_ref, gain_two_ref, bias_two_ref, norm_ref,
+    gain_ref, bias_ref, g_ref, cot_ref, mix_from, q_from, k_from, v_from, o_from, conv_from,
+    encoded_out, out_ref, sums_two_out, sums_one_out,
+    mix, q_weight, k_weight, v_weight, o_weight, weight,
+    hat_two, slope_two, trunk, row_hat, mixed, hat_one, slope_one, q_rows, k_rows, v_rows,
+    a_rows, gq_rows, gv_rows, gk_rows,
+    x_part, y_part, x_got, y_got, y_turned, score, slope, total_vk, oq, vk,
+    oq_got, vk_got, from_core, to_z, from_z, summed,
+    line_two, plane_two, line_one, plane_one, middle, padded, low, high,
+    head_send, head_recv, sum_send, sum_recv, move_send, move_recv, own_sem
 ):
-    sems = (send_sem, recv_sem)
-    spread_heads(q_ref, k_ref, v_ref, g_ref, x_got, y_got, x_part, y_part, sems)
-    attend_rows(x_got, y_got, oq, vk, y_turned, score, slope, total)
+    heads = (head_send, head_recv)
+    sums = (sum_send, sum_recv)
+    moves = (move_send, move_recv)
+    total_rows = ROWS * lax.axis_size("seq") * lax.axis_size("batch")
+    kind = x_ref.dtype
+    full = jnp.float32
+    barrier, count = greet_all()
+    count += greet_attention(barrier)
+    loads = [
+        pltpu.make_async_copy(source, target, own_sem.at[i])
+        for i, (source, target) in enumerate(
+            (
+                (mix_from, mix),
+                (q_from, q_weight),
+                (k_from, k_weight),
+                (v_from, v_weight),
+                (o_from, o_weight),
+                (conv_from, weight),
+            )
+        )
+    ]
+    for load in loads:
+        load.start()
+    mean_two = stats_two_ref[0:1, :] / total_rows
+    scale_two = lax.rsqrt(stats_two_ref[1:2, :] / total_rows - mean_two * mean_two + EPS)
+    hat = (hidden_ref[...] - mean_two) * scale_two
+    pre = hat * gain_two_ref[...][None, :] + bias_two_ref[...][None, :]
+    hat_two[...] = hat
+    loads[0].wait()
+    trunk[...] = (
+        x_ref[...].astype(full)
+        + jnp.dot(gelu_value(pre).astype(kind), mix[...], preferred_element_type=full)
+    ).astype(kind)
+    rows = trunk[...].astype(full)
+    centered = rows - jnp.mean(rows, axis=-1, keepdims=True)
+    row_scale = lax.rsqrt(jnp.mean(centered * centered, axis=-1, keepdims=True) + EPS)
+    row_hat[...] = centered * row_scale
+    norm_gain = norm_ref[...][None, :]
+    normed = (row_hat[...] * norm_gain).astype(kind)
+    for load, table, place in (
+        (loads[3], v_weight, v_rows),
+        (loads[2], k_weight, k_rows),
+        (loads[1], q_weight, q_rows),
+    ):
+        load.wait()
+        place[...] = jnp.dot(normed, table[...], preferred_element_type=full).astype(kind)
+    pl.semaphore_wait(barrier, count)
+
+    mean, scale = stats_one_ref[0:1, :], stats_one_ref[1:2, :]
+    gain_one = gain_ref[...][None, :]
+
+    def recall():
+        slope_two[...] = gelu_slope(hat_two[...] * gain_two_ref[...][None, :] + bias_two_ref[...][None, :])
+        hat_one[...] = (x_ref[...].astype(full) - mean) * scale
+        slope_one[...] = gelu_slope(hat_one[...] * gain_one + bias_ref[...][None, :])
+
+    def encode():
+        loads[4].wait()
+        encoded_out[...] = (
+            trunk[...].astype(full) + jnp.dot(a_rows[...], o_weight[...], preferred_element_type=full)
+        ).astype(kind)
+        mixed[...] = lax.dot_general(gq_rows[...], q_weight[...], SIDE, preferred_element_type=full)
+
+    spread_heads(q_rows, k_rows, v_rows, g_ref, x_got, y_got, x_part, y_part, heads, recall)
+    attend_rows(x_got, y_got, oq, vk, y_turned, score, slope, total_vk)
     collect_heads(
-        oq, vk, a_ref, gq_ref, gv_ref, gk_ref, oq_got, vk_got, from_core, to_z, from_z, summed, sems
-    )
-
-
-def attention(queries, keys, values, grad_out):
+        oq, vk, a_rows, gq_rows, gv_rows, gk_rows, oq_got, vk_got, from_core, to_z, from_z, summed,
+        heads, encode
+    )
+    grad_normed = (
+        mixed[...]
+        + lax.dot_general(gk_rows[...], k_weight[...], SIDE, preferred_element_type=full)
+        + lax.dot_general(gv_rows[...], v_weight[...], SIDE, preferred_element_type=full)
+    )
+    hats = row_hat[...]
+    norm_part = jnp.sum(grad_normed * hats, axis=0, keepdims=True)
+    grad_hat = grad_normed * norm_gain
+    mixed[...] = cot_ref[...].astype(full) + row_scale * (
+        grad_hat
+        - jnp.mean(grad_hat, axis=-1, keepdims=True)
+        - hats * jnp.mean(grad_hat * hats, axis=-1, keepdims=True)
+    )
+    grad_two = (
+        lax.dot_general(mixed[...].astype(kind), mix[...], SIDE, preferred_element_type=full)
+        * slope_two[...]
+    )
+    mid_width = grad_two.shape[1]
+    place = line_place()
+    line_two[place] = jnp.concatenate(
+        [
+            jnp.sum(grad_two, axis=0, keepdims=True),
+            jnp.sum(grad_two * hat_two[...], axis=0, keepdims=True),
+            norm_part[:, :mid_width],
+            norm_part[:, mid_width:],
+        ],
+        axis=0,
+    )
+    started = line_send(line_two, sums, 0)
+    plane_started = plane_send(line_two, plane_two, started, sums, 0)
+    total = plane_sum(plane_two, plane_started)
+    sums_two_out[...] = total
+    hidden_grad = (
+        gain_two_ref[...][None, :]
+        * scale_two
+        * (grad_two - total[0:1, :] / total_rows - hat_two[...] * total[1:2, :] / total_rows)
+    ).astype(kind)
+    for window in range(2):
+        middle[window] = hidden_grad[window * 64 : window * 64 + 64, :]
+        padded[window, 16:80, :] = hidden_grad[window * 64 : window * 64 + 64, :]
+    halos = halo_send(middle, low, high, moves, 0)
+    loads[5].wait()
+    grad_act = None
+    for tap, half, start, size in (TAP_PARTS[1], TAP_PARTS[2], TAP_PARTS[0], TAP_PARTS[3]):
+        if tap == 0:
+            halo_fill(padded, low, high, halos)
+        first = 0 if half == 0 or tap == 2 else 384
+        term = lax.dot_general(
+            tap_rows(padded, 16 * (2 - tap))[:, first : first + size],
+            weight[half, :, start : start + size],
+            SIDE,
+            preferred_element_type=jnp.float32,
+        )
+        grad_act = term if grad_act is None else grad_act + term
+    grad_pre = grad_act * slope_one[...]
+    line_one[place] = stacked([grad_pre, grad_pre * hat_one[...]])
+    line_again = line_send(line_one, sums, LINE + PLANE)
+    plane_again = plane_send(line_one, plane_one, line_again, sums, LINE + PLANE)
+    total = plane_sum(plane_one, plane_again)
+    sums_one_out[...] = total
+    grad_rows = (
+        gain_one
+        * scale
+        * (grad_pre - total[0:1, :] / total_rows - hat_one[...] * total[1:2, :] / total_rows)
+    )
+    out_ref[...] = (mixed[...] + grad_rows).astype(out_ref.dtype)
+    for copy in started + plane_started + halos + line_again + plane_again:
+        copy.wait_send()
+
+
+def back(
+    rows_in, hidden, stats_one, stats_two, gain_two, bias_two, norm_gain, gain_one, bias_one,
+    grad_out, cot, mix_full, query_weight, key_weight, value_weight, out_weight, conv_full
+):
     vmem = pl.BlockSpec(memory_space=pltpu.VMEM)
-    kind = queries.dtype
+    anywhere = pl.BlockSpec(memory_space=pl.ANY)
+    kind, full = rows_in.dtype, jnp.float32
+    width, mid_width = rows_in.shape[1], hidden.shape[1]
     piece = (16, 64, WIDE)
     count = 4 * 16 * 64
+    sems = 2 * (LINE + PLANE)
+    weights = (mix_full, query_weight, key_weight, value_weight, out_weight, conv_full)
+    scratch = [(table.shape, kind) for table in weights]
+    scratch += [((ROWS, mid_width), full)] * 2 + [((ROWS, width), kind)] + [((ROWS, width), full)] * 4
+    scratch += [((ROWS, H * KD), kind)] * 2 + [((ROWS, H * VD), kind)] * 2
+    scratch += [((ROWS, H * KD), kind), ((ROWS, H * VD), kind), ((ROWS, H * KD), kind)]
+    scratch += [(piece, kind)] * 3 + [((2, 2) + piece, kind), ((WIDE, count), kind)]
+    scratch += [((count, QUERY_BLOCK), full)] * 2 + [((count, WIDE), full)]
+    scratch += [(piece, kind), ((2, 2) + piece, kind), (piece, kind), (piece, kind)]
+    scratch += [((2,) + piece, kind)] + [(piece, kind)] * 3
+    scratch += [((LINE, 4, mid_width), full), ((PLANE, 4, mid_width), full)]
+    scratch += [((LINE, 2, width), full), ((PLANE, 2, width), full)]
+    scratch += [((2, 64, mid_width), kind), ((2, 96, mid_width), kind)] + [((2, 16, mid_width), kind)] * 2
+    dma = pltpu.SemaphoreType.DMA
     return pl.pallas_call(
-        attention_kernel,
+        back_kernel,
         out_shape=[
-            jax.ShapeDtypeStruct((ROWS, H * VD), kind),
-            jax.ShapeDtypeStruct((ROWS, H * KD), kind),
-            jax.ShapeDtypeStruct((ROWS, H * VD), kind),
-            jax.ShapeDtypeStruct((ROWS, H * KD), kind),
+            jax.ShapeDtypeStruct((ROWS, width), kind),
+            jax.ShapeDtypeStruct((ROWS, width), kind),
+            jax.ShapeDtypeStruct((4, mid_width), full),
+            jax.ShapeDtypeStruct((2, width), full),
         ],
-        in_specs=[vmem] * 4,
+        in_specs=[vmem] * 11 + [anywhere] * 6,
         out_specs=[vmem] * 4,
-        scratch_shapes=[
-            pltpu.VMEM(piece, kind),
-            pltpu.VMEM(piece, kind),
-            pltpu.VMEM(piece, kind),
-            pltpu.VMEM((2, 2) + piece, kind),
-            pltpu.VMEM((WIDE, count), kind),
-            pltpu.VMEM((count, QUERY_BLOCK), jnp.float32),
-            pltpu.VMEM((count, QUERY_BLOCK), jnp.float32),
-            pltpu.VMEM((count, WIDE), jnp.float32),
-            pltpu.VMEM(piece, kind),
-            pltpu.VMEM((2, 2) + piece, kind),
-            pltpu.VMEM(piece, kind),
-            pltpu.VMEM(piece, kind),
-            pltpu.VMEM((2,) + piece, kind),
-            pltpu.VMEM(piece, kind),
-            pltpu.VMEM(piece, kind),
-            pltpu.VMEM(piece, kind),
-            pltpu.SemaphoreType.DMA((128,)),
-            pltpu.SemaphoreType.DMA((128,)),
-        ],
+        scratch_shapes=[pltpu.VMEM(shape, held) for shape, held in scratch]
+        + [dma((128,)), dma((128,)), dma((sems,)), dma((sems,)), dma((1, 2)), dma((1, 2)), dma((6,))],
         compiler_params=pltpu.CompilerParams(
-            collective_id=3, has_side_effects=True, vmem_limit_bytes=56 * 1024 * 1024
+            collective_id=2, has_side_effects=True, vmem_limit_bytes=62 * 1024 * 1024
         ),
-        name="attention",
-    )(queries, keys, values, grad_out)
+        name="back",
+    )(
+        rows_in, hidden, stats_one, stats_two, gain_two, bias_two, norm_gain, gain_one, bias_one,
+        grad_out, cot, *weights
+    )
 
 
 def on_device(
@@ -751,74 +809,32 @@
     cotangent,
 ):
     windows_here, local_bins, model_width = inputs.shape
-    devices = lax.axis_size("seq")
     local_count = windows_here * local_bins
-    total_rows = local_count * devices * lax.axis_size("batch")
     rows_in = inputs.reshape(local_count, model_width)
-    inputs_flat = rows_in.astype(jnp.float32)
     cot_flat = cotangent.reshape(local_count, model_width)
-    gain_one, bias_one = first_gain[None, :], first_bias[None, :]
     conv_full, mix_full, hidden, stats_one, stats_two, grad_out = front(
-        rows_in, conv_weight, mix_weight, gain_one, bias_one, cot_flat, out_weight
-    )
-    sum_two, square_two = stats_two[0], stats_two[1]
-    mean_two = sum_two / total_rows
-    scale_two = lax.rsqrt(square_two / total_rows - mean_two * mean_two + EPS)
-    hat_two = (hidden - mean_two) * scale_two
-    pre_two = hat_two * second_gain + second_bias
-    act_two = gelu_value(pre_two).astype(jnp.bfloat16)
-    mixed_rows = inputs_flat + jnp.dot(act_two, mix_full, preferred_element_type=jnp.float32)
-    trunk_rows = rounded(mixed_rows)
-    row_mean = jnp.mean(trunk_rows, axis=-1, keepdims=True)
-    centered = trunk_rows - row_mean
-    row_scale = lax.rsqrt(jnp.mean(centered * centered, axis=-1, keepdims=True) + EPS)
-    row_hat = centered * row_scale
-    normed = (row_hat * norm_gain).astype(jnp.bfloat16)
-    queries = jnp.dot(normed, query_weight, preferred_element_type=jnp.float32).astype(jnp.bfloat16)
-    keys_local = jnp.dot(normed, key_weight, preferred_element_type=jnp.float32).astype(
-        jnp.bfloat16
-    )
-    values_local = jnp.dot(normed, value_weight, preferred_element_type=jnp.float32).astype(
-        jnp.bfloat16
-    )
-    attended_rows, grad_query_rows, grad_value_rows, grad_key_rows = attention(
-        queries, keys_local, values_local, grad_out
-    )
-    encoded = (
-        (trunk_rows + jnp.dot(attended_rows, out_weight, preferred_element_type=jnp.float32))
-        .astype(jnp.bfloat16)
-        .reshape(windows_here, local_bins, model_width)
-    )
-    grad_normed = jnp.dot(grad_query_rows, query_weight.T, preferred_element_type=jnp.float32)
-    grad_normed = grad_normed + jnp.dot(
-        grad_key_rows, key_weight.T, preferred_element_type=jnp.float32
-    )
-    grad_normed = grad_normed + jnp.dot(
-        grad_value_rows, value_weight.T, preferred_element_type=jnp.float32
-    )
-    norm_gain_part = jnp.sum(grad_normed * row_hat, axis=0)
-    grad_hat = grad_normed * norm_gain
-    grad_trunk = row_scale * (
-        grad_hat
-        - jnp.mean(grad_hat, axis=-1, keepdims=True)
-        - row_hat * jnp.mean(grad_hat * row_hat, axis=-1, keepdims=True)
-    )
-    grad_mixed = cot_flat.astype(jnp.float32) + grad_trunk
-    grad_low = grad_mixed.astype(jnp.bfloat16)
-    grad_act_two = jnp.dot(grad_low, mix_full.T, preferred_element_type=jnp.float32)
-    grad_pre_two = grad_act_two * gelu_slope(pre_two)
-    grad_rows, sums_two, sums_one = tail(
-        grad_pre_two,
-        hat_two,
-        (second_gain * scale_two)[None, :],
-        norm_gain_part.reshape(2, -1),
+        rows_in, conv_weight, mix_weight, first_gain, first_bias, cot_flat, out_weight
+    )
+    encoded_rows, grad_rows, sums_two, sums_one = back(
         rows_in,
+        hidden,
         stats_one,
-        gain_one,
-        bias_one,
-        grad_mixed,
+        stats_two,
+        second_gain,
+        second_bias,
+        norm_gain,
+        first_gain,
+        first_bias,
+        grad_out,
+        cot_flat,
+        mix_full,
+        query_weight,
+        key_weight,
+        value_weight,
+        out_weight,
         conv_full,
     )
+    encoded = encoded_rows.reshape(windows_here, local_bins, model_width)
     grad_inputs = grad_rows.reshape(windows_here, local_bins, model_width)
     grad_second_bias, grad_second_gain = sums_two[0], sums_two[1]
     grad_norm_gain = sums_two[2:4].reshape(-1)

time: 187 us -> 175 us (0.936)
  matrix products: 15.3 us -> 0 us
  Pallas kernels: 152 us -> 157 us
    dot_general x9 -> x0, matrix products: 15.3 us -> none  [the longest x1 4.05 us: on_device(): jnp.dot(attended_rows, out_weight, preferred_element_type=jnp.float32)]
    pallas_call x2 -> x1, Pallas kernels: 94 us -> 99.1 us  [back(): pl.pallas_call(back_kernel, out_shape=[jax.ShapeDtypeStruct((ROWS, width)...]
    broadcast_in_dim x3 -> x0, local copies, waits for them, and re-layouts: 2.1 us -> none  [the longest x2 1.52 us: on_device(): gain_one, bias_one = (first_gain[None, :], first_bias[None, :])]
    unnamed x47 -> x24, local copies, waits for them, and re-layouts: 12 us -> 12.7 us
where the time goes in v2:
time: 175 us
  Pallas kernels  157 us (90%)
  local copies, waits for them, and re-layouts  16.9 us (10%)
    pallas_call x1, Pallas kernels, back(): pl.pallas_call(back_kernel, out_shape=[jax.ShapeDtypeStruct((ROWS, width)...  99.1 us
    pallas_call x1, Pallas kernels, front(): pl.pallas_call(front_kernel, out_shape=[jax.ShapeDtypeStruct((2, 4, 4, 2,...  58 us
    unnamed x24, local copies, waits for them, and re-layouts  12.7 us

profile of v2, /device:TPU:1, one launch (start us, length us, event | category | flops | bytes accessed | tf_op | source)
XLA Modules:
  0.0 174.6 jit_solution(14232221110575953971)
XLA Ops:
  0.6 0.0 copy-start.1
  0.6 1.0 copy-done.1
  1.6 0.0 copy-start.2
  1.6 1.0 copy-done.2
  2.6 0.0 copy-start.5
  2.6 0.9 copy-done.5
  3.5 0.0 copy-start.6
  3.5 0.8 copy-done.6
  4.3 0.0 copy-start.7
  4.3 0.7 copy-done.7
  5.0 0.0 copy-start.8
  5.0 0.7 copy-done.8
  5.7 58.0 %front.1 = (bf16[2,4,4,2,48,1152]{5,4,3,2,1,0:T(8,128)(2,1)}, bf16[768,1536]{1,0:T(8,128)(2,1)S(1)}, f32[128,768]{1,0:T(8,128)S(1)}, f32[2,1536]{1,0:T(2,128)S(1...) custom-call(bf16[128,1536]{1,0:T(8,128)(2,1)S(1)} %bitcast.6, bf16[24,2304]{1,0:T(8,128)(2,1)S(1)} %copy-done.5, ...), custom_call_target="tpu_custom_call" | custom-call | tf_op jit(solution)/shard_map/front/pallas_call | solution.py:332
  63.7 0.0 copy-start
  63.8 1.5 copy-done
  65.2 0.0 copy-start.3
  65.2 0.7 copy-done.3
  66.0 0.0 copy-start.4
  66.0 0.7 copy-done.4
  66.7 0.0 copy-start.9
  66.7 0.6 copy-done.9
  67.3 0.0 copy-start.10
  67.3 0.6 copy-done.10
  67.9 99.1 %back.1 = (bf16[128,1536]{1,0:T(8,128)(2,1)}, bf16[128,1536]{1,0:T(8,128)(2,1)}, f32[4,768]{1,0:T(4,128)}, f32[2,1536]{1,0:T(2,128)}) custom-call(bf16[128,1536]{1,0:T(8,128)(2,1)} %bitcast.5, f32[128,768]{1,0:T(8,128)} %copy-done.3, f32[2,1536]{1,0:T(2,128)} %copy-done.9, f32[2,768]{1,0:T(2,128)} %copy-done.10, f32[768]{0:T(1024)} %gain_two_ref.1, ...), custom_call_target="tpu_custom_call" | custom-call | tf_op jit(solution)/shard_map/back/pallas_call | solution.py:774
  167.0 0.7 slice.19
  167.7 1.4 slice_reduce_fusion.2
  169.1 0.6 reshape.37
  169.7 1.4 slice_reduce_fusion
  171.1 1.8 %copy.22 = bf16[2,64,1536]{2,1,0:T(8,128)(2,1)} copy(bf16[2,64,1536]{2,1,0:T(8,128)(2,1)} %bitcast.11) | data formatting | bytes 786432
  172.9 1.8 %copy.23 = bf16[2,64,1536]{2,1,0:T(8,128)(2,1)} copy(bf16[2,64,1536]{2,1,0:T(8,128)(2,1)} %bitcast.10) | data formatting | bytes 786432
Async XLA Ops:
  0.6 1.0 copy-start.1
  1.6 1.0 copy-start.2
  2.6 0.9 copy-start.5
  3.5 0.8 copy-start.6
  4.3 0.7 copy-start.7
  5.0 0.7 copy-start.8
  63.7 1.5 copy-start
  65.2 0.7 copy-start.3
  66.0 0.7 copy-start.4
  66.7 0.6 copy-start.9
  67.3 0.6 copy-start.10

commit v3 on v2

--- a/solution.py
+++ b/solution.py
@@ -144,8 +144,8 @@
 SIDE = (((1,), (1,)), ((), ()))
 def front_kernel(
     x_from, conv_from, mix_from, gain_ref, bias_ref, cot_from, out_weight_ref,
-    conv_out, mix_out, hidden_out, stats_one_out, stats_two_out, grad_out,
-    line_one, plane_one, line_two, plane_two, conv_other, mix_other, mix_land, middle, padded,
+    conv_to, mix_to, hidden_out, stats_one_out, stats_two_out, grad_out,
+    conv_out, mix_out, line_one, plane_one, line_two, plane_two, conv_other, mix_other, mix_land, middle, padded,
     low, high, weight, x_ref, conv_ref, mix_ref, cot_ref, sum_send, sum_recv, move_send, move_recv, own_sem
 ):
     seq = lax.axis_index("seq")
@@ -291,6 +291,8 @@
     finish(0)
     for copy in across[0]:
         copy.wait_recv()
+    stores = [pltpu.make_async_copy(conv_out, conv_to, own_sem.at[5])]
+    stores[0].start()
     terms = {}
     for tap, half, start, size in TAP_PARTS:
         part = conv_out[half, :, :, :, :, start : start + size].reshape(-1, size)
@@ -312,12 +314,16 @@
                 pair = [mix_land[half, i, j, k].astype(jnp.float32) for k in range(2)]
                 columns = slice(half * widths[1], half * widths[1] + widths[1])
                 mix_out[start : start + 48, columns] = jnp.concatenate(pair, axis=0).astype(mix_out.dtype)
+    stores.append(pltpu.make_async_copy(mix_out, mix_to, own_sem.at[6]))
+    stores[1].start()
     stats_two_out[...] = plane_sum(plane_two, plane_again)
     ended = started + to_x + spread_out + halos + plane_started + line_again + plane_again
     for kind in range(2):
         ended += blocks[kind] + across[kind]
     for copy in ended:
         copy.wait_send()
+    for copy in stores:
+        copy.wait()
 
 
 def front(inputs, conv_weight, mix_weight, gain, bias, cot, out_weight):
@@ -340,8 +346,10 @@
             jax.ShapeDtypeStruct((ROWS, out_weight.shape[0]), kind),
         ],
         in_specs=[anywhere] * 3 + [vmem] * 2 + [anywhere] * 2,
-        out_specs=[vmem] * 6,
+        out_specs=[anywhere] * 2 + [vmem] * 4,
         scratch_shapes=[
+            pltpu.VMEM((2, 4, 4, 2, 2 * conv_rows, wide // 2), kind),
+            pltpu.VMEM((64 * mix_rows, width), kind),
             pltpu.VMEM((LINE, 2, width), full),
             pltpu.VMEM((PLANE, 2, width), full),
             pltpu.VMEM((LINE, 2, mid_width), full),
@@ -362,10 +370,10 @@
             pltpu.SemaphoreType.DMA((sems,)),
             pltpu.SemaphoreType.DMA((26, 2)),
             pltpu.SemaphoreType.DMA((26, 2)),
-            pltpu.SemaphoreType.DMA((5,)),
+            pltpu.SemaphoreType.DMA((7,)),
         ],
         compiler_params=pltpu.CompilerParams(
-            collective_id=1, has_side_effects=True, vmem_limit_bytes=48 * 1024 * 1024
+            collective_id=1, has_side_effects=True, vmem_limit_bytes=62 * 1024 * 1024
         ),
         name="front",
     )(inputs, conv_weight, mix_weight, gain, bias, cot, out_weight)
@@ -581,19 +589,24 @@
         for part in chunks:
             probs = score[part, :] * share
             prob_low = probs.astype(jnp.bfloat16)
-            grads = (probs * (slope[part, :] - center) * key_scale).astype(jnp.bfloat16)
+            grads = (probs * (slope[part, :] - center)).astype(jnp.bfloat16)
             out = out + jnp.dot(y_turned[:, part], prob_low, preferred_element_type=jnp.float32)
             back = back + jnp.dot(y_turned[:, part], grads, preferred_element_type=jnp.float32)
             for_values = jnp.dot(prob_low, x_block, preferred_element_type=jnp.float32)
             for_keys = jnp.dot(grads, x_block, preferred_element_type=jnp.float32)
             total[part, :] += jnp.where(low_keys, for_values, for_keys)
         low_rows = lax.broadcasted_iota(jnp.int32, out.shape, 0) < LOW
-        turned = jnp.where(low_rows, out, back).T
+        turned = jnp.where(low_rows, out, back * key_scale).T
         oq_ref[rows] = turned.reshape(4, 64, WIDE).astype(oq_ref.dtype)
         return carry
 
     lax.fori_loop(0, x_ref.shape[0] // 4, block, 0)
-    vk_ref[...] = total[...].reshape(vk_ref.shape).astype(vk_ref.dtype)
+    low_keys = lax.broadcasted_iota(jnp.int32, (CHUNK, WIDE), 1) < LOW
+    for part in chunks:
+        quarter = part.start // CHUNK
+        grads = total[part, :]
+        grads = jnp.where(low_keys, grads, grads * key_scale).astype(vk_ref.dtype)
+        vk_ref[quarter // 2, quarter % 2] = grads.reshape(vk_ref.shape[2:])
 
 
 def back_kernel(

time: 175 us -> 165 us (0.943)
  local copies, waits for them, and re-layouts: 16.9 us -> 7.67 us
    unnamed x24 -> x2, local copies, waits for them, and re-layouts: 12.7 us -> 3.53 us
where the time goes in v3:
time: 165 us
  Pallas kernels  156 us (95%)
  local copies, waits for them, and re-layouts  7.67 us (5%)
    pallas_call x1, Pallas kernels, back(): pl.pallas_call(back_kernel, out_shape=[jax.ShapeDtypeStruct((ROWS, width)...  98.8 us
    pallas_call x1, Pallas kernels, front(): pl.pallas_call(front_kernel, out_shape=[jax.ShapeDtypeStruct((2, 4, 4, 2,...  57.6 us
    unnamed x2, local copies, waits for them, and re-layouts  3.53 us

profile of v3, /device:TPU:1, one launch (start us, length us, event | category | flops | bytes accessed | tf_op | source)
XLA Modules:
  0.0 164.8 jit_solution(17482676963692718765)
XLA Ops:
  0.6 57.6 %front.1 = (bf16[2,4,4,2,48,1152]{5,4,3,2,1,0:T(8,128)(2,1)}, bf16[768,1536]{1,0:T(8,128)(2,1)}, f32[128,768]{1,0:T(8,128)}, f32[2,1536]{1,0:T(2,128)}, f32[2,768]{1,0:T(2,128)}, /*index=5*/bf16[128,1536]{1,0:T(8,128)(2,1)}) custom-call(bf16[128,1536]{1,0:T(8,128)(2,1)} %bitcast.6, bf16[24,2304]{1,0:T(8,128)(2,1)} %conv_from.1, bf16[12,1536]{1,0:T(8,128)(2,1)} %mix_from.1, ...), custom_call_target="tpu_custom_call" | custom-call | tf_op jit(solution)/shard_map/front/pallas_call | solution.py:338
  58.2 98.8 %back.1 = (bf16[128,1536]{1,0:T(8,128)(2,1)}, bf16[128,1536]{1,0:T(8,128)(2,1)}, f32[4,768]{1,0:T(4,128)}, f32[2,1536]{1,0:T(2,128)}) custom-call(bf16[128,1536]{1,0:T(8,128)(2,1)} %bitcast.7, f32[128,768]{1,0:T(8,128)} %get-tuple-element.17.hidden_ref, f32[2,1536]{1,0:T(2,128)} %get-tuple-element.18.stats_one_ref, ...), custom_call_target="tpu_custom_call" | custom-call | tf_op jit(solution)/shard_map/back/pallas_call | solution.py:787
  157.1 0.7 slice.19
  157.8 1.4 slice_reduce_fusion.2
  159.2 0.6 reshape.37
  159.8 1.4 slice_reduce_fusion
  161.2 1.8 %copy.22 = bf16[2,64,1536]{2,1,0:T(8,128)(2,1)} copy(bf16[2,64,1536]{2,1,0:T(8,128)(2,1)} %bitcast.11) | data formatting | bytes 786432
  163.0 1.8 %copy.23 = bf16[2,64,1536]{2,1,0:T(8,128)(2,1)} copy(bf16[2,64,1536]{2,1,0:T(8,128)(2,1)} %bitcast.10) | data formatting | bytes 786432

commit v4 on v3

--- a/solution.py
+++ b/solution.py
@@ -139,7 +139,7 @@
     return lax.optimization_barrier(values.astype(jnp.bfloat16)).astype(jnp.float32)
 
 
-CHUNK = 1024
+CHUNK = 256
 QUERY_BLOCK = 256
 SIDE = (((1,), (1,)), ((), ()))
 def front_kernel(
@@ -551,8 +551,8 @@
     chunks = [slice(start, start + CHUNK) for start in range(0, keys, CHUNK)]
 
     def key_rows(part):
-        quarter = part.start // CHUNK
-        return y_ref[quarter // 2, quarter % 2].reshape(CHUNK, WIDE)
+        quarter, first = part.start // 1024, part.start % 1024 // 64
+        return y_ref[quarter // 2, quarter % 2, first : first + CHUNK // 64].reshape(CHUNK, WIDE)
 
     key_scale = KD ** (-0.5)
     for part in chunks:
@@ -603,10 +603,11 @@
     lax.fori_loop(0, x_ref.shape[0] // 4, block, 0)
     low_keys = lax.broadcasted_iota(jnp.int32, (CHUNK, WIDE), 1) < LOW
     for part in chunks:
-        quarter = part.start // CHUNK
+        quarter, first = part.start // 1024, part.start % 1024 // 64
         grads = total[part, :]
         grads = jnp.where(low_keys, grads, grads * key_scale).astype(vk_ref.dtype)
-        vk_ref[quarter // 2, quarter % 2] = grads.reshape(vk_ref.shape[2:])
+        pieces = slice(first, first + CHUNK // 64)
+        vk_ref[quarter // 2, quarter % 2, pieces] = grads.reshape(CHUNK // 64, 64, WIDE)
 
 
 def back_kernel(
@@ -806,6 +807,51 @@
     )
 
 
+def finish_kernel(
+    encoded_from, grad_from, two_ref, one_ref,
+    encoded_to, grad_to, gain_one, bias_one, gain_two, bias_two, gain_norm, own_sem
+):
+    copies = [
+        pltpu.make_async_copy(encoded_from, encoded_to, own_sem.at[0]),
+        pltpu.make_async_copy(grad_from, grad_to, own_sem.at[1]),
+    ]
+    for copy in copies:
+        copy.start()
+    mid_width = two_ref.shape[1]
+    bias_one[...] = one_ref[0, :]
+    gain_one[...] = one_ref[1, :]
+    bias_two[...] = two_ref[0, :]
+    gain_two[...] = two_ref[1, :]
+    gain_norm[0:mid_width] = two_ref[2, :]
+    gain_norm[mid_width : 2 * mid_width] = two_ref[3, :]
+    for copy in copies:
+        copy.wait()
+
+
+def finish(encoded, grad_inputs, sums_two, sums_one):
+    vmem = pl.BlockSpec(memory_space=pltpu.VMEM)
+    anywhere = pl.BlockSpec(memory_space=pl.ANY)
+    width, mid_width = sums_one.shape[1], sums_two.shape[1]
+    full = jnp.float32
+    return pl.pallas_call(
+        finish_kernel,
+        out_shape=[
+            jax.ShapeDtypeStruct(encoded.shape, encoded.dtype),
+            jax.ShapeDtypeStruct(grad_inputs.shape, grad_inputs.dtype),
+            jax.ShapeDtypeStruct((width,), full),
+            jax.ShapeDtypeStruct((width,), full),
+            jax.ShapeDtypeStruct((mid_width,), full),
+            jax.ShapeDtypeStruct((mid_width,), full),
+            jax.ShapeDtypeStruct((2 * mid_width,), full),
+        ],
+        in_specs=[anywhere] * 2 + [vmem] * 2,
+        out_specs=[anywhere] * 2 + [vmem] * 5,
+        scratch_shapes=[pltpu.SemaphoreType.DMA((2,))],
+        compiler_params=pltpu.CompilerParams(vmem_limit_bytes=62 * 1024 * 1024),
+        name="finish",
+    )(encoded, grad_inputs, sums_two, sums_one)
+
+
 def on_device(
     inputs,
     conv_weight,
@@ -847,20 +893,8 @@
         out_weight,
         conv_full,
     )
-    encoded = encoded_rows.reshape(windows_here, local_bins, model_width)
-    grad_inputs = grad_rows.reshape(windows_here, local_bins, model_width)
-    grad_second_bias, grad_second_gain = sums_two[0], sums_two[1]
-    grad_norm_gain = sums_two[2:4].reshape(-1)
-    grad_first_bias, grad_first_gain = sums_one[0], sums_one[1]
-    return (
-        encoded,
-        grad_inputs,
-        grad_first_gain,
-        grad_first_bias,
-        grad_second_gain,
-        grad_second_bias,
-        grad_norm_gain,
-    )
+    whole = (windows_here, local_bins, model_width)
+    return finish(encoded_rows.reshape(whole), grad_rows.reshape(whole), sums_two, sums_one)
 
 
 def solution(mesh):

time: 165 us -> 183 us (1.11)
  Pallas kernels: 156 us -> 182 us
  local copies, waits for them, and re-layouts: 7.67 us -> 0 us
    pallas_call x0 -> x1, Pallas kernels: none -> 26.3 us  [finish(): pl.pallas_call(finish_kernel, out_shape=[jax.ShapeDtypeStruct(encoded.sha...]
    unnamed x2 -> x0, local copies, waits for them, and re-layouts: 3.53 us -> none
    slice x3 -> x0, local copies, waits for them, and re-layouts: 3.53 us -> none  [the longest x1 1.42 us: on_device(): grad_first_bias, grad_first_gain = (sums_one[0], sums_one[1])]
where the time goes in v4:
time: 183 us; the launch traced here: 182 us
  Pallas kernels  182 us (99%)
    pallas_call x1, Pallas kernels, back(): pl.pallas_call(back_kernel, out_shape=[jax.ShapeDtypeStruct((ROWS, width)...  97.6 us
    pallas_call x1, Pallas kernels, front(): pl.pallas_call(front_kernel, out_shape=[jax.ShapeDtypeStruct((2, 4, 4, 2,...  57.6 us
    pallas_call x1, Pallas kernels, finish(): pl.pallas_call(finish_kernel, out_shape=[jax.ShapeDtypeStruct(encoded.sha...  26.3 us

profile of v4, /device:TPU:1, one launch (start us, length us, event | category | flops | bytes accessed | tf_op | source)
XLA Modules:
  0.0 182.3 jit_solution(1040652145187824314)
XLA Ops:
  0.6 57.6 %front.1 = (bf16[2,4,4,2,48,1152]{5,4,3,2,1,0:T(8,128)(2,1)}, bf16[768,1536]{1,0:T(8,128)(2,1)}, f32[128,768]{1,0:T(8,128)}, f32[2,1536]{1,0:T(2,128)}, f32[2,768]{1,0:T(2,128)}, /*index=5*/bf16[128,1536]{1,0:T(8,128)(2,1)}) custom-call(bf16[128,1536]{1,0:T(8,128)(2,1)} %bitcast.6, bf16[24,2304]{1,0:T(8,128)(2,1)} %conv_from.1, bf16[12,1536]{1,0:T(8,128)(2,1)} %mix_from.1, ...), custom_call_target="tpu_custom_call" | custom-call | tf_op jit(solution)/shard_map/front/pallas_call | solution.py:338
  58.2 97.6 %back.1 = (bf16[128,1536]{1,0:T(8,128)(2,1)}, bf16[128,1536]{1,0:T(8,128)(2,1)}, f32[4,768]{1,0:T(4,128)}, f32[2,1536]{1,0:T(2,128)}) custom-call(bf16[128,1536]{1,0:T(8,128)(2,1)} %bitcast.7, f32[128,768]{1,0:T(8,128)} %get-tuple-element.17.hidden_ref, f32[2,1536]{1,0:T(2,128)} %get-tuple-element.18.stats_one_ref, ...), custom_call_target="tpu_custom_call" | custom-call | tf_op jit(solution)/shard_map/back/pallas_call | solution.py:788
  155.9 26.3 %finish.1 = (bf16[2,64,1536]{2,1,0:T(8,128)(2,1)}, bf16[2,64,1536]{2,1,0:T(8,128)(2,1)}, f32[1536]{0:T(1024)}, f32[1536]{0:T(1024)}, f32[768]{0:T(1024)}, /*index=5*/f32[768]{0:T(1024)}, f32[1536]{0:T(1024)}) custom-call(bf16[2,64,1536]{2,1,0:T(8,128)(2,1)} %bitcast.10, bf16[2,64,1536]{2,1,0:T(8,128)(2,1)} %bitcast.11, f32[4,768]{1,0:T(4,128)} %get-tuple-element.25.two_ref, ...), custom_call_target="tpu_custom_call" | custom-call | tf_op jit(solution)/shard_map/finish/pallas_call | solution.py:836

commit v5 on v4

--- a/solution.py
+++ b/solution.py
@@ -643,7 +643,7 @@
             )
         )
     ]
-    for load in loads:
+    for load in loads[:4]:
         load.start()
     mean_two = stats_two_ref[0:1, :] / total_rows
     scale_two = lax.rsqrt(stats_two_ref[1:2, :] / total_rows - mean_two * mean_two + EPS)
@@ -674,6 +674,8 @@
     gain_one = gain_ref[...][None, :]
 
     def recall():
+        for load in loads[4:]:
+            load.start()
         slope_two[...] = gelu_slope(hat_two[...] * gain_two_ref[...][None, :] + bias_two_ref[...][None, :])
         hat_one[...] = (x_ref[...].astype(full) - mean) * scale
         slope_one[...] = gelu_slope(hat_one[...] * gain_one + bias_ref[...][None, :])
@@ -809,14 +811,10 @@
 
 def finish_kernel(
     encoded_from, grad_from, two_ref, one_ref,
-    encoded_to, grad_to, gain_one, bias_one, gain_two, bias_two, gain_norm, own_sem
+    encoded_to, grad_to, gain_one, bias_one, gain_two, bias_two, gain_norm
 ):
-    copies = [
-        pltpu.make_async_copy(encoded_from, encoded_to, own_sem.at[0]),
-        pltpu.make_async_copy(grad_from, grad_to, own_sem.at[1]),
-    ]
-    for copy in copies:
-        copy.start()
+    encoded_to[...] = encoded_from[...]
+    grad_to[...] = grad_from[...]
     mid_width = two_ref.shape[1]
     bias_one[...] = one_ref[0, :]
     gain_one[...] = one_ref[1, :]
@@ -824,13 +822,10 @@
     gain_two[...] = two_ref[1, :]
     gain_norm[0:mid_width] = two_ref[2, :]
     gain_norm[mid_width : 2 * mid_width] = two_ref[3, :]
-    for copy in copies:
-        copy.wait()
 
 
 def finish(encoded, grad_inputs, sums_two, sums_one):
     vmem = pl.BlockSpec(memory_space=pltpu.VMEM)
-    anywhere = pl.BlockSpec(memory_space=pl.ANY)
     width, mid_width = sums_one.shape[1], sums_two.shape[1]
     full = jnp.float32
     return pl.pallas_call(
@@ -844,9 +839,8 @@
             jax.ShapeDtypeStruct((mid_width,), full),
             jax.ShapeDtypeStruct((2 * mid_width,), full),
         ],
-        in_specs=[anywhere] * 2 + [vmem] * 2,
-        out_specs=[anywhere] * 2 + [vmem] * 5,
-        scratch_shapes=[pltpu.SemaphoreType.DMA((2,))],
+        in_specs=[vmem] * 4,
+        out_specs=[vmem] * 7,
         compiler_params=pltpu.CompilerParams(vmem_limit_bytes=62 * 1024 * 1024),
         name="finish",
     )(encoded, grad_inputs, sums_two, sums_one)

time: 183 us -> 158 us (0.86)
  Pallas kernels: 182 us -> 157 us
    pallas_call x1, Pallas kernels: 26.3 us -> 2.04 us  [finish(): pl.pallas_call(finish_kernel, out_shape=[jax.ShapeDtypeStruct(encoded.sha...]
where the time goes in v5:
time: 158 us
  Pallas kernels  157 us (99%)
    pallas_call x1, Pallas kernels, back(): pl.pallas_call(back_kernel, out_shape=[jax.ShapeDtypeStruct((ROWS, width)...  97.6 us
    pallas_call x1, Pallas kernels, front(): pl.pallas_call(front_kernel, out_shape=[jax.ShapeDtypeStruct((2, 4, 4, 2,...  57.6 us

profile of v5, /device:TPU:1, one launch (start us, length us, event | category | flops | bytes accessed | tf_op | source)
XLA Modules:
  0.0 157.9 jit_solution(15429013651871038519)
XLA Ops:
  0.6 57.6 %front.1 = (bf16[2,4,4,2,48,1152]{5,4,3,2,1,0:T(8,128)(2,1)}, bf16[768,1536]{1,0:T(8,128)(2,1)}, f32[128,768]{1,0:T(8,128)}, f32[2,1536]{1,0:T(2,128)}, f32[2,768]{1,0:T(2,128)}, /*index=5*/bf16[128,1536]{1,0:T(8,128)(2,1)}) custom-call(bf16[128,1536]{1,0:T(8,128)(2,1)} %bitcast.6, bf16[24,2304]{1,0:T(8,128)(2,1)} %conv_from.1, bf16[12,1536]{1,0:T(8,128)(2,1)} %mix_from.1, ...), custom_call_target="tpu_custom_call" | custom-call | tf_op jit(solution)/shard_map/front/pallas_call | solution.py:338
  58.2 97.6 %back.1 = (bf16[128,1536]{1,0:T(8,128)(2,1)}, bf16[128,1536]{1,0:T(8,128)(2,1)}, f32[4,768]{1,0:T(4,128)}, f32[2,1536]{1,0:T(2,128)}) custom-call(bf16[128,1536]{1,0:T(8,128)(2,1)} %bitcast.7, f32[128,768]{1,0:T(8,128)} %get-tuple-element.17.hidden_ref, f32[2,1536]{1,0:T(2,128)} %get-tuple-element.18.stats_one_ref, ...), custom_call_target="tpu_custom_call" | custom-call | tf_op jit(solution)/shard_map/back/pallas_call | solution.py:790
  155.9 2.0 %finish.1 = (bf16[2,64,1536]{2,1,0:T(8,128)(2,1)}, bf16[2,64,1536]{2,1,0:T(8,128)(2,1)}, f32[1536]{0:T(1024)}, f32[1536]{0:T(1024)}, f32[768]{0:T(1024)}, /*index=5*/f32[768]{0:T(1024)}, f32[1536]{0:T(1024)}) custom-call(bf16[2,64,1536]{2,1,0:T(8,128)(2,1)} %bitcast.10, bf16[2,64,1536]{2,1,0:T(8,128)(2,1)} %bitcast.11, f32[4,768]{1,0:T(4,128)} %get-tuple-element.25.two_ref, ...), custom_call_target="tpu_custom_call" | custom-call | tf_op jit(solution)/shard_map/finish/pallas_call | solution.py:831

commit v6 on v5

--- a/solution.py
+++ b/solution.py
@@ -287,8 +287,8 @@
     halo_fill(padded, low, high, halos)
 
     relay(0)
+    finish(0)
     launch(1)
-    finish(0)
     for copy in across[0]:
         copy.wait_recv()
     stores = [pltpu.make_async_copy(conv_out, conv_to, own_sem.at[5])]

time: 158 us -> 159 us (level)
    pallas_call x1, Pallas kernels: 97.6 us -> 99.5 us  [back(): pl.pallas_call(back_kernel, out_shape=[jax.ShapeDtypeStruct((ROWS, width)...]
where the time goes in v6:
time: 159 us
  Pallas kernels  158 us (99%)
    pallas_call x1, Pallas kernels, back(): pl.pallas_call(back_kernel, out_shape=[jax.ShapeDtypeStruct((ROWS, width)...  99.5 us
    pallas_call x1, Pallas kernels, front(): pl.pallas_call(front_kernel, out_shape=[jax.ShapeDtypeStruct((2, 4, 4, 2,...  56.9 us

profile of v6, /device:TPU:1, one launch (start us, length us, event | category | flops | bytes accessed | tf_op | source)
XLA Modules:
  0.0 159.1 jit_solution(17207100001892647063)
XLA Ops:
  0.6 56.9 %front.1 = (bf16[2,4,4,2,48,1152]{5,4,3,2,1,0:T(8,128)(2,1)}, bf16[768,1536]{1,0:T(8,128)(2,1)}, f32[128,768]{1,0:T(8,128)}, f32[2,1536]{1,0:T(2,128)}, f32[2,768]{1,0:T(2,128)}, /*index=5*/bf16[128,1536]{1,0:T(8,128)(2,1)}) custom-call(bf16[128,1536]{1,0:T(8,128)(2,1)} %bitcast.6, bf16[24,2304]{1,0:T(8,128)(2,1)} %conv_from.1, bf16[12,1536]{1,0:T(8,128)(2,1)} %mix_from.1, ...), custom_call_target="tpu_custom_call" | custom-call | tf_op jit(solution)/shard_map/front/pallas_call | solution.py:338
  57.5 99.5 %back.1 = (bf16[128,1536]{1,0:T(8,128)(2,1)}, bf16[128,1536]{1,0:T(8,128)(2,1)}, f32[4,768]{1,0:T(4,128)}, f32[2,1536]{1,0:T(2,128)}) custom-call(bf16[128,1536]{1,0:T(8,128)(2,1)} %bitcast.7, f32[128,768]{1,0:T(8,128)} %get-tuple-element.17.hidden_ref, f32[2,1536]{1,0:T(2,128)} %get-tuple-element.18.stats_one_ref, ...), custom_call_target="tpu_custom_call" | custom-call | tf_op jit(solution)/shard_map/back/pallas_call | solution.py:790
  157.0 2.0 %finish.1 = (bf16[2,64,1536]{2,1,0:T(8,128)(2,1)}, bf16[2,64,1536]{2,1,0:T(8,128)(2,1)}, f32[1536]{0:T(1024)}, f32[1536]{0:T(1024)}, f32[768]{0:T(1024)}, /*index=5*/f32[768]{0:T(1024)}, f32[1536]{0:T(1024)}) custom-call(bf16[2,64,1536]{2,1,0:T(8,128)(2,1)} %bitcast.10, bf16[2,64,1536]{2,1,0:T(8,128)(2,1)} %bitcast.11, f32[4,768]{1,0:T(4,128)} %get-tuple-element.25.two_ref, ...), custom_call_target="tpu_custom_call" | custom-call | tf_op jit(solution)/shard_map/finish/pallas_call | solution.py:831

commit v7 on v5

--- a/solution.py
+++ b/solution.py
@@ -676,9 +676,6 @@
     def recall():
         for load in loads[4:]:
             load.start()
-        slope_two[...] = gelu_slope(hat_two[...] * gain_two_ref[...][None, :] + bias_two_ref[...][None, :])
-        hat_one[...] = (x_ref[...].astype(full) - mean) * scale
-        slope_one[...] = gelu_slope(hat_one[...] * gain_one + bias_ref[...][None, :])
 
     def encode():
         loads[4].wait()
@@ -686,6 +683,7 @@
             trunk[...].astype(full) + jnp.dot(a_rows[...], o_weight[...], preferred_element_type=full)
         ).astype(kind)
         mixed[...] = lax.dot_general(gq_rows[...], q_weight[...], SIDE, preferred_element_type=full)
+        slope_two[...] = gelu_slope(hat_two[...] * gain_two_ref[...][None, :] + bias_two_ref[...][None, :])
 
     spread_heads(q_rows, k_rows, v_rows, g_ref, x_got, y_got, x_part, y_part, heads, recall)
     attend_rows(x_got, y_got, oq, vk, y_turned, score, slope, total_vk)
@@ -722,7 +720,9 @@
         axis=0,
     )
     started = line_send(line_two, sums, 0)
+    hat_one[...] = (x_ref[...].astype(full) - mean) * scale
     plane_started = plane_send(line_two, plane_two, started, sums, 0)
+    slope_one[...] = gelu_slope(hat_one[...] * gain_one + bias_ref[...][None, :])
     total = plane_sum(plane_two, plane_started)
     sums_two_out[...] = total
     hidden_grad = (

time: 158 us -> 158 us (level)
  no operation moved by 1% of the time
where the time goes in v7:
time: 158 us
  Pallas kernels  157 us (99%)
    pallas_call x1, Pallas kernels, back(): pl.pallas_call(back_kernel, out_shape=[jax.ShapeDtypeStruct((ROWS, width)...  97.6 us
    pallas_call x1, Pallas kernels, front(): pl.pallas_call(front_kernel, out_shape=[jax.ShapeDtypeStruct((2, 4, 4, 2,...  57.6 us

profile of v7, /device:TPU:1, one launch (start us, length us, event | category | flops | bytes accessed | tf_op | source)
XLA Modules:
  0.0 157.9 jit_solution(11441462999840431050)
XLA Ops:
  0.6 57.6 %front.1 = (bf16[2,4,4,2,48,1152]{5,4,3,2,1,0:T(8,128)(2,1)}, bf16[768,1536]{1,0:T(8,128)(2,1)}, f32[128,768]{1,0:T(8,128)}, f32[2,1536]{1,0:T(2,128)}, f32[2,768]{1,0:T(2,128)}, /*index=5*/bf16[128,1536]{1,0:T(8,128)(2,1)}) custom-call(bf16[128,1536]{1,0:T(8,128)(2,1)} %bitcast.6, bf16[24,2304]{1,0:T(8,128)(2,1)} %conv_from.1, bf16[12,1536]{1,0:T(8,128)(2,1)} %mix_from.1, ...), custom_call_target="tpu_custom_call" | custom-call | tf_op jit(solution)/shard_map/front/pallas_call | solution.py:338
  58.2 97.6 %back.1 = (bf16[128,1536]{1,0:T(8,128)(2,1)}, bf16[128,1536]{1,0:T(8,128)(2,1)}, f32[4,768]{1,0:T(4,128)}, f32[2,1536]{1,0:T(2,128)}) custom-call(bf16[128,1536]{1,0:T(8,128)(2,1)} %bitcast.7, f32[128,768]{1,0:T(8,128)} %get-tuple-element.17.hidden_ref, f32[2,1536]{1,0:T(2,128)} %get-tuple-element.18.stats_one_ref, ...), custom_call_target="tpu_custom_call" | custom-call | tf_op jit(solution)/shard_map/back/pallas_call | solution.py:790
  155.8 2.0 %finish.1 = (bf16[2,64,1536]{2,1,0:T(8,128)(2,1)}, bf16[2,64,1536]{2,1,0:T(8,128)(2,1)}, f32[1536]{0:T(1024)}, f32[1536]{0:T(1024)}, f32[768]{0:T(1024)}, /*index=5*/f32[768]{0:T(1024)}, f32[1536]{0:T(1024)}) custom-call(bf16[2,64,1536]{2,1,0:T(8,128)(2,1)} %bitcast.10, bf16[2,64,1536]{2,1,0:T(8,128)(2,1)} %bitcast.11, f32[4,768]{1,0:T(4,128)} %get-tuple-element.25.two_ref, ...), custom_call_target="tpu_custom_call" | custom-call | tf_op jit(solution)/shard_map/finish/pallas_call | solution.py:831
